TPU v7x, 512 devices: a whole 4x8x8 slice. The times are simulated.
512 devices in a mesh: frame: 32 (over z, y_lo, core), row: 16 (over y_hi, x).
Axes of the slice: x: 4, y: 8 (y_hi: 4, y_lo: 2; y = y_hi * 2 + y_lo), z: 8, core: 2. Of those that a mesh axis runs over, the one named last changes fastest.
Arguments:
- queries: bfloat16 [32, 2048, 2560], P('frame', 'row'), may hold values from -12 to 12
- key_states: bfloat16 [32, 2048, 2560], P('frame', 'row'), may hold values from -12 to 12
- value_states: bfloat16 [32, 2048, 2560], P('frame', 'row'), may hold values from -6 to 6
- radial_mask: int32 [5, 32, 5], replicated, may hold values from 0 to 1, as said below
Outputs:
- attended: bfloat16 [32, 2048, 2560], P('frame', 'row')
Inputs may be any that keep to these rules, and one draw needn't show every extreme that they name: radial_mask[e, b, j] is 1 only where |e - 2| + |j - 2| <= 2, and radial_mask[2, b, 2] is 1 for every block b.
All inputs are finite; a program needn't handle non-finite values.
Results may differ from a plain program's by a relative error of at most 0.0054.
Values may be sent and summed in bfloat16 or wider, within the bound.
No kernel may reach another device: no remote copies, remote signals or barrier semaphores. Data moves between devices by JAX's collectives and lax.ppermute only.
A program may use at most 64 MiB of HBM per device.

v0:
```python
import jax
import jax.numpy as jnp
from jax import lax
from jax.sharding import PartitionSpec as P

HDIM = 128
BLK = 64
REACH = 2


NEG_FILL = -1e30


def padded(block, sides, width):
    for axis, dim in sides:
        count = lax.axis_size(axis)
        forward = [(i, i + 1) for i in range(count - 1)]
        backward = [(target, source) for source, target in forward]
        low = lax.ppermute(
            lax.slice_in_dim(block, block.shape[dim] - width, None, axis=dim), axis, forward
        )
        high = lax.ppermute(lax.slice_in_dim(block, 0, width, axis=dim), axis, backward)
        block = jnp.concatenate([low, block, high], axis=dim)
    return block


def passed_along(shard, axis, by):
    length = lax.axis_size(axis)
    pairs = [(i, i + by) for i in range(length) if 0 <= i + by < length]
    return lax.ppermute(shard, axis, pairs)


def block_allowed(radial_mask, frame_offset, halo_blocks, query_first, own_blocks, frame_valid):
    offset_count = radial_mask.shape[2]
    reach_blocks = offset_count // 2
    total_blocks = radial_mask.shape[1]
    mask_rows = lax.dynamic_slice_in_dim(
        radial_mask[reach_blocks + frame_offset], query_first, own_blocks, 0
    )
    key_blocks = own_blocks + 2 * halo_blocks
    query_index = jnp.arange(own_blocks, dtype=jnp.int32)[:, None]
    key_index = jnp.arange(key_blocks, dtype=jnp.int32)[None, :]
    offset_index = reach_blocks + key_index - halo_blocks - query_index
    onehot = offset_index[:, :, None] == jnp.arange(offset_count, dtype=jnp.int32)[None, None, :]
    chosen = jnp.sum(jnp.where(onehot, mask_rows[:, None, :], 0), axis=2)
    global_block = query_first - halo_blocks + key_index
    inside = (global_block >= 0) & (global_block < total_blocks)
    return (chosen > 0) & inside & frame_valid


def attend(carry_state, query_heads, key_value, allowed, block_rows):
    running_max, running_sum, running_out = carry_state
    length, head_count, head_depth = query_heads.shape
    key_count = key_value.shape[1]
    key_heads = key_value[0].reshape(key_count, head_count, head_depth)
    value_heads = key_value[1].reshape(key_count, head_count, head_depth)
    scores = jnp.einsum(
        "qhd,khd->hqk", query_heads, key_heads, preferred_element_type=jnp.float32
    ) * head_depth ** (-0.5)
    score_tiles = scores.reshape(
        head_count, length // block_rows, block_rows, key_count // block_rows, block_rows
    )
    score_tiles = jnp.where(allowed[None, :, None, :, None], score_tiles, NEG_FILL)
    scores = score_tiles.reshape(head_count, length, key_count)
    new_max = jnp.maximum(running_max, jnp.max(scores, axis=2))
    weights = jnp.exp(scores - new_max[:, :, None])
    rescale = jnp.exp(running_max - new_max)
    running_sum = running_sum * rescale + jnp.sum(weights, axis=2)
    update = jnp.einsum(
        "hqk,khd->qhd",
        weights.astype(jnp.bfloat16),
        value_heads,
        preferred_element_type=jnp.float32,
    )
    running_out = running_out * jnp.transpose(rescale)[:, :, None] + update
    return (new_max, running_sum, running_out)


def shards(queries, key_states, value_states, radial_mask):
    length = queries.shape[1]
    width_total = queries.shape[2]
    head_count = width_total // HDIM
    own_blocks = length // BLK
    frame_at = lax.axis_index("frame")
    row_at = lax.axis_index("row")
    frame_total = lax.axis_size("frame")
    query_first = row_at * own_blocks
    stacked = jnp.stack([key_states, value_states])
    widened = padded(stacked, (("row", 2),), REACH * BLK)
    corner_rows = (REACH - 1) * BLK
    trimmed = widened[:, :, BLK : BLK + length + 2 * corner_rows]
    neighbours = padded(trimmed, (("frame", 1),), 1)
    before_near = neighbours[:, 0]
    after_near = neighbours[:, 2]
    distant = [passed_along(stacked[:, 0], "frame", 2 * direction) for direction in (1, -1)]

    def allowed_for(frame_offset, halo_blocks):
        frame_valid = (frame_at + frame_offset >= 0) & (frame_at + frame_offset < frame_total)
        return block_allowed(
            radial_mask, frame_offset, halo_blocks, query_first, own_blocks, frame_valid
        )

    groups = [
        (widened[:, 0], allowed_for(0, REACH)),
        (before_near, allowed_for(-1, REACH - 1)),
        (after_near, allowed_for(1, REACH - 1)),
        (distant[0], allowed_for(-2, 0)),
        (distant[1], allowed_for(2, 0)),
    ]
    query_heads = queries[0].reshape(length, head_count, HDIM)
    carry_state = (
        jnp.full((head_count, length), NEG_FILL, jnp.float32),
        jnp.zeros((head_count, length), jnp.float32),
        jnp.zeros((length, head_count, HDIM), jnp.float32),
    )
    carry_state = attend(carry_state, query_heads, groups[0][0], groups[0][1], BLK)
    for first_index in (1, 3):
        joined = jnp.concatenate([groups[first_index][0], groups[first_index + 1][0]], axis=1)
        joined_allowed = jnp.concatenate(
            [groups[first_index][1], groups[first_index + 1][1]], axis=1
        )
        carry_state = attend(carry_state, query_heads, joined, joined_allowed, BLK)
    result = carry_state[2] / jnp.transpose(carry_state[1])[:, :, None]
    return result.reshape(1, length, width_total).astype(jnp.bfloat16)


def solution(mesh):
    in_specs = (P("frame", "row", None), P("frame", "row", None), P("frame", "row", None), P())
    out_specs = P("frame", "row", None)
    return jax.shard_map(shards, mesh=mesh, in_specs=in_specs, out_specs=out_specs, check_vma=False)
```

profile of v0, /device:TPU:223, one launch (start us, length us, event | category | flops | bytes accessed | tf_op | source)
XLA Modules:
  0.0 195.9 jit_solution(9192156441116447690)
XLA Ops:
  0.0 1.4 copy.47
  1.4 1.4 copy.46
  2.8 1.7 fusion.62
  4.5 2.4 %collective-permute-start.1 = (bf16[2,1,128,2560]{2,3,1,0:T(8,128)(2,1)}, bf16[2,1,128,2560]{2,3,1,0:T(8,128)(2,1)}, u32[]{:S(2)}, u32[]{:S(2)}) collective-permute-start(bf16[2,1,128,2560]{2,3,1,0:T(8,128)(2,1)} %get-tuple-element.22), channel_id=1, source_target_pairs={{1,0},{2,1},{3,2},{4,3},{5,4},{6,5},{7,6},{8,7},{9,8},{10,9},{11,1... | collective-permute-start | bytes 3932168 | tf_op jit(solution)/shard_map/ppermute | solution.py:22
  7.0 7.0 %collective-permute-start = (bf16[2,1,128,2560]{2,3,1,0:T(8,128)(2,1)}, bf16[2,1,128,2560]{2,3,1,0:T(8,128)(2,1)}, u32[]{:S(2)}, u32[]{:S(2)}) collective-permute-start(bf16[2,1,128,2560]{2,3,1,0:T(8,128)(2,1)} %get-tuple-element.22), channel_id=1, source_target_pairs={{0,1},{1,2},{2,3},{3,4},{4,5},{5,6},{6,7},{7,8},{8,9},{9,10},{10,1... | collective-permute-start | bytes 3932168 | tf_op jit(solution)/shard_map/ppermute | solution.py:19
  14.0 5.1 %collective-permute-start.4 = (bf16[2,128,2560]{1,2,0:T(8,128)(2,1)}, bf16[2,128,2560]{1,2,0:T(8,128)(2,1)}, u32[]{:S(2)}, u32[]{:S(2)}) collective-permute-start(bf16[2,128,2560]{1,2,0:T(8,128)(2,1)} %get-tuple-element.21), channel_id=1, source_target_pairs={{0,32},{16,48},{32,64},{48,80},{64,96},{80,112},{96,128},{112,144}... | collective-permute-start | bytes 3932168 | tf_op jit(solution)/shard_map/ppermute | solution.py:30
  19.1 1.9 collective-permute-start.5
  22.3 1.4 copy.48
  25.4 15.5 %collective-permute-done.1 = bf16[2,1,128,2560]{2,3,1,0:T(8,128)(2,1)} collective-permute-done((bf16[2,1,128,2560]{2,3,1,0:T(8,128)(2,1)}, bf16[2,1,128,2560]{2,3,1,0:T(8,128)(2,1)}, u32[]{:S(2)}, u32[]{:S(2)}) %collective-permute-start.1) | collective-permute-done | bytes 1310752 | tf_op jit(solution)/shard_map/ppermute | solution.py:22
  40.9 28.5 %collective-permute-done = bf16[2,1,128,2560]{2,3,1,0:T(8,128)(2,1)} collective-permute-done((bf16[2,1,128,2560]{2,3,1,0:T(8,128)(2,1)}, bf16[2,1,128,2560]{2,3,1,0:T(8,128)(2,1)}, u32[]{:S(2)}, u32[]{:S(2)}) %collective-permute-start) | collective-permute-done | bytes 1310752 | tf_op jit(solution)/shard_map/ppermute | solution.py:19
  69.4 2.0 %pad_maximum_fusion = bf16[2,1,384,2560]{2,3,1,0:T(8,128)(2,1)S(1)} fusion(bf16[2,1,128,2560]{2,3,1,0:T(8,128)(2,1)} %collective-permute-done.1, bf16[1,1,128,2560]{2,3,1,0:T(8,128)(2,1)S(1)} %bitcast.143, bf16[1,1,128,2560]{2,3,1,0:T(8,128)(2,1)S(1)} %bitcast.145, bf16[2,1,128,2560]{2,3,1,0:T(8,128)(2,1)} %collective-permute-done), kind=kLoop, calls=%fused_computation.7 | loop fusion | flops 15728640 | bytes 7864320 | tf_op jit(solution)/shard_map/concatenate | solution.py:23
  71.4 1.3 slice_bitcast_fusion
  72.7 8.4 %collective-permute-start.2 = (bf16[2,1,256,2560]{2,3,0,1:T(8,128)(2,1)S(1)}, bf16[2,1,256,2560]{2,3,0,1:T(8,128)(2,1)S(1)}, u32[]{:S(2)}, u32[]{:S(2)}) collective-permute-start(bf16[2,1,256,2560]{2,3,0,1:T(8,128)(2,1)S(1)} %get-tuple-element.17), channel_id=1, source_target_pairs={{0,16},{16,32},{32,48},{48,64},{64,80},{80,96},{96,112},{112,128},... | collective-permute-start | bytes 7864328 | tf_op jit(solution)/shard_map/ppermute | solution.py:19
  81.1 2.1 %collective-permute-start.3 = (bf16[2,1,256,2560]{2,3,1,0:T(8,128)(2,1)S(1)}, bf16[2,1,256,2560]{2,3,1,0:T(8,128)(2,1)S(1)}, u32[]{:S(2)}, u32[]{:S(2)}) collective-permute-start(bf16[2,1,256,2560]{2,3,1,0:T(8,128)(2,1)S(1)} %get-tuple-element.18), channel_id=1, source_target_pairs={{16,0},{32,16},{48,32},{64,48},{80,64},{96,80},{112,96},{128,112},... | collective-permute-start | bytes 7864328 | tf_op jit(solution)/shard_map/ppermute | solution.py:22
  83.2 15.3 %collective-permute-done.4 = bf16[2,128,2560]{1,2,0:T(8,128)(2,1)} collective-permute-done((bf16[2,128,2560]{1,2,0:T(8,128)(2,1)}, bf16[2,128,2560]{1,2,0:T(8,128)(2,1)}, u32[]{:S(2)}, u32[]{:S(2)}) %collective-permute-start.4) | collective-permute-done | bytes 1310752 | tf_op jit(solution)/shard_map/ppermute | solution.py:30
  98.5 1.5 constant_dynamic-update-slice_fusion.1
  100.0 29.5 %collective-permute-done.5 = bf16[2,128,2560]{1,2,0:T(8,128)(2,1)S(1)} collective-permute-done((bf16[2,128,2560]{1,2,0:T(8,128)(2,1)}, bf16[2,128,2560]{1,2,0:T(8,128)(2,1)S(1)}, u32[]{:S(2)}, u32[]{:S(2)}) %collective-permute-start.5) | collective-permute-done | bytes 1310752 | tf_op jit(solution)/shard_map/ppermute | solution.py:30
  129.5 0.3 constant_dynamic-update-slice_fusion
  130.0 0.7 fusion.15
  130.6 0.4 fusion.66
  131.0 1.0 fusion.5
  132.1 5.0 %collective-permute-done.2 = bf16[2,1,256,2560]{2,3,0,1:T(8,128)(2,1)S(1)} collective-permute-done((bf16[2,1,256,2560]{2,3,0,1:T(8,128)(2,1)S(1)}, bf16[2,1,256,2560]{2,3,0,1:T(8,128)(2,1)S(1)}, u32[]{:S(2)}, u32[]{:S(2)}) %collective-permute-start.2) | collective-permute-done | bytes 2621472 | tf_op jit(solution)/shard_map/ppermute | solution.py:19
  137.1 49.8 %collective-permute-done.3 = bf16[2,1,256,2560]{2,3,1,0:T(8,128)(2,1)S(1)} collective-permute-done((bf16[2,1,256,2560]{2,3,1,0:T(8,128)(2,1)S(1)}, bf16[2,1,256,2560]{2,3,1,0:T(8,128)(2,1)S(1)}, u32[]{:S(2)}, u32[]{:S(2)}) %collective-permute-start.3) | collective-permute-done | bytes 2621472 | tf_op jit(solution)/shard_map/ppermute | solution.py:22
  186.8 0.4 fusion.8
  187.2 1.3 fusion.2
  188.5 1.1 fusion
  189.6 1.6 fusion.25
  191.2 0.6 fusion.13
  191.8 0.8 fusion.3
  192.6 1.3 fusion.39
  193.9 0.9 fusion.42
  194.9 1.1 copy.65
  (38 shorter events, 2.9 us)
Async XLA Ops:
  1.4 19.7 %copy-start = (s32[5,32,5]{1,2,0:T(8,128)S(1)}, s32[5,32,5]{1,2,0:T(8,128)}, u32[]{:S(2)}) copy-start(s32[5,32,5]{1,2,0:T(8,128)} %param.7) | copy-start | bytes 9604
  4.5 36.4 %collective-permute-start.1 = (bf16[2,1,128,2560]{2,3,1,0:T(8,128)(2,1)}, bf16[2,1,128,2560]{2,3,1,0:T(8,128)(2,1)}, u32[]{:S(2)}, u32[]{:S(2)}) collective-permute-start(bf16[2,1,128,2560]{2,3,1,0:T(8,128)(2,1)} %get-tuple-element.22), channel_id=1, source_target_pairs={{1,0},{2,1},{3,2},{4,3},{5,4},{6,5},{7,6},{8,7},{9,8},{10,9},{11,1... | collective-permute-start | bytes 3932168 | tf_op jit(solution)/shard_map/ppermute | solution.py:22
  7.0 62.4 %collective-permute-start = (bf16[2,1,128,2560]{2,3,1,0:T(8,128)(2,1)}, bf16[2,1,128,2560]{2,3,1,0:T(8,128)(2,1)}, u32[]{:S(2)}, u32[]{:S(2)}) collective-permute-start(bf16[2,1,128,2560]{2,3,1,0:T(8,128)(2,1)} %get-tuple-element.22), channel_id=1, source_target_pairs={{0,1},{1,2},{2,3},{3,4},{4,5},{5,6},{6,7},{7,8},{8,9},{9,10},{10,1... | collective-permute-start | bytes 3932168 | tf_op jit(solution)/shard_map/ppermute | solution.py:19
  14.0 84.4 %collective-permute-start.4 = (bf16[2,128,2560]{1,2,0:T(8,128)(2,1)}, bf16[2,128,2560]{1,2,0:T(8,128)(2,1)}, u32[]{:S(2)}, u32[]{:S(2)}) collective-permute-start(bf16[2,128,2560]{1,2,0:T(8,128)(2,1)} %get-tuple-element.21), channel_id=1, source_target_pairs={{0,32},{16,48},{32,64},{48,80},{64,96},{80,112},{96,128},{112,144}... | collective-permute-start | bytes 3932168 | tf_op jit(solution)/shard_map/ppermute | solution.py:30
  19.1 110.3 %collective-permute-start.5 = (bf16[2,128,2560]{1,2,0:T(8,128)(2,1)}, bf16[2,128,2560]{1,2,0:T(8,128)(2,1)S(1)}, u32[]{:S(2)}, u32[]{:S(2)}) collective-permute-start(bf16[2,128,2560]{1,2,0:T(8,128)(2,1)} %get-tuple-element.21), channel_id=1, source_target_pairs={{32,0},{48,16},{64,32},{80,48},{96,64},{112,80},{128,96},{144,112}... | collective-permute-start | bytes 3932168 | tf_op jit(solution)/shard_map/ppermute | solution.py:30
  72.7 64.3 %collective-permute-start.2 = (bf16[2,1,256,2560]{2,3,0,1:T(8,128)(2,1)S(1)}, bf16[2,1,256,2560]{2,3,0,1:T(8,128)(2,1)S(1)}, u32[]{:S(2)}, u32[]{:S(2)}) collective-permute-start(bf16[2,1,256,2560]{2,3,0,1:T(8,128)(2,1)S(1)} %get-tuple-element.17), channel_id=1, source_target_pairs={{0,16},{16,32},{32,48},{48,64},{64,80},{80,96},{96,112},{112,128},... | collective-permute-start | bytes 7864328 | tf_op jit(solution)/shard_map/ppermute | solution.py:19
  81.1 105.7 %collective-permute-start.3 = (bf16[2,1,256,2560]{2,3,1,0:T(8,128)(2,1)S(1)}, bf16[2,1,256,2560]{2,3,1,0:T(8,128)(2,1)S(1)}, u32[]{:S(2)}, u32[]{:S(2)}) collective-permute-start(bf16[2,1,256,2560]{2,3,1,0:T(8,128)(2,1)S(1)} %get-tuple-element.18), channel_id=1, source_target_pairs={{16,0},{32,16},{48,32},{64,48},{80,64},{96,80},{112,96},{128,112},... | collective-permute-start | bytes 7864328 | tf_op jit(solution)/shard_map/ppermute | solution.py:22
where the time goes:
time: 196 us
  waiting for transfers between devices  144 us (73%)
  starting transfers between devices  27 us (14%)
  local copies, waits for them, and re-layouts  11.1 us (6%)
  other arithmetic  7.23 us (4%)
  matrix products  6.8 us (3%)
    ppermute x2, waiting for transfers between devices, padded(): lax.ppermute(lax.slice_in_dim(block, 0, width, axis=dim), axis, backward)  65.3 us
    ppermute x2, waiting for transfers between devices, passed_along(): return lax.ppermute(shard, axis, pairs)  44.7 us
    ppermute x2, waiting for transfers between devices, padded(): lax.ppermute(lax.slice_in_dim(block, block.shape[dim] - width, None, axis...  33.5 us
    ppermute x2, starting transfers between devices, padded(): lax.ppermute(lax.slice_in_dim(block, block.shape[dim] - width, None, axis...  15.4 us
    ppermute x2, starting transfers between devices, passed_along(): return lax.ppermute(shard, axis, pairs)  7.02 us
    unnamed x6, local copies, waits for them, and re-layouts  5.78 us
    ppermute x2, starting transfers between devices, padded(): lax.ppermute(lax.slice_in_dim(block, 0, width, axis=dim), axis, backward)  4.55 us
  transfers between devices with their start and end apart: 6, of which 6 were waited for; matrix products, arithmetic and copies ran while one was open for 6% of the time, Pallas kernels for 0%

commit v1 on v0

v1 whole, which is shorter than its diff:
```python
import functools

import jax
import jax.numpy as jnp
import numpy as np
from jax import lax
from jax.experimental import pallas as pl
from jax.experimental.pallas import tpu as pltpu
from jax.sharding import PartitionSpec as P

HDIM = 128
BLK = 64
REACH = 2
NEG = -1e30
SCALE = HDIM ** -0.5 * 1.4426950408889634
AXES = ("frame", "row")
GROUP = 4
XN = 4
VMEM = pl.BlockSpec(memory_space=pltpu.VMEM)
SMEM = pl.BlockSpec(memory_space=pltpu.SMEM)
ANY = pl.BlockSpec(memory_space=pl.ANY)
FRAME_STEPS = (-2, -1, 0, 1, 2)
HALO_STEPS = (-1, 0, 1)
OWN_KEYS = 2 * BLK * len(FRAME_STEPS)


def pairs_of(frames, rows, target):
    pairs = []
    for frame in range(frames):
        for row in range(rows):
            to = target(frame, row)
            if to is not None and 0 <= to[0] < frames and 0 <= to[1] < rows:
                pairs.append((frame * rows + row, to[0] * rows + to[1]))
    return pairs


def key_block_table():
    own = [(step, block) for step in FRAME_STEPS for block in (0, 1)]
    halo = []
    for step in HALO_STEPS:
        reach = REACH - abs(step)
        halo += [(step, block) for block in range(-reach, 0)]
        halo += [(step, block) for block in range(2, 2 + reach)]
    return own + halo


def bias_of(radial_mask, frame_first, row_at, frame_total):
    table = key_block_table()
    offsets = 2 * REACH + 1
    pick = np.zeros((2, len(table), offsets * 2 * offsets), np.float32)
    for query in range(2):
        for at, (step, block) in enumerate(table):
            offset = block - query + REACH
            if 0 <= offset < offsets:
                pick[query, at, ((step + REACH) * 2 + query) * offsets + offset] = 1.0
    rows = lax.dynamic_slice_in_dim(radial_mask, row_at * 2, 2, 1)
    chosen = jnp.sum(jnp.asarray(pick) * rows.reshape(1, 1, -1).astype(jnp.float32), axis=2)
    steps = jnp.asarray(np.array([s for s, _ in table], np.int32))
    blocks = jnp.asarray(np.array([b for _, b in table], np.int32)) + row_at * 2
    inside = (blocks >= 0) & (blocks < radial_mask.shape[1])
    frames = frame_first + jnp.arange(GROUP, dtype=jnp.int32)[:, None] + steps[None, :]
    valid = (frames >= 0) & (frames < frame_total) & inside[None, :]
    allowed = (chosen[None] > 0) & valid[:, None, :]
    bias = jnp.where(allowed, 0.0, NEG).astype(jnp.float32)
    return jnp.repeat(bias, BLK, axis=2)


def pack_kernel(at_ref, q_ref, k_ref, v_ref, out0, out1, out2, out3, sems):
    me = at_ref[0]
    outs = (out0, out1, out2, out3)
    width = out0.shape[2]
    copies = []
    for slot in (1, 2, 3, 0):
        columns = pl.ds(pl.multiple_of((me ^ slot) * width, HDIM), width)
        for which, source in enumerate((k_ref, v_ref, q_ref)):
            copies.append(
                pltpu.make_async_copy(
                    source.at[:, columns], outs[slot].at[which], sems.at[slot, which]
                )
            )
    for copy in copies:
        copy.start()
    for copy in copies:
        copy.wait()


def unpack_kernel(in_ref, out_ref, sems):
    width = in_ref.shape[2]
    copies = [
        pltpu.make_async_copy(
            in_ref.at[part], out_ref.at[:, pl.ds(part * width, width)], sems.at[part]
        )
        for part in range(GROUP)
    ]
    for copy in copies:
        copy.start()
    for copy in copies:
        copy.wait()


def corner_kernel(own_pair, at_ref, *refs):
    me, x_at = at_ref[0], at_ref[1]
    out, sems = refs[-2], refs[-1]
    lows, highs = refs[: (len(refs) - 2) // 2], refs[(len(refs) - 2) // 2 : -2]
    length = lows[0].shape[2]
    if own_pair:
        slot = jnp.where(me < 2, me, 3 - me)
    else:
        slot = jnp.where(me < 2, 1 - me, me - 2)

    def from_low(source):
        rows = pl.ds(length - BLK, BLK)
        return pltpu.make_async_copy(source.at[slot, :, rows], out.at[:, pl.ds(0, BLK)], sems.at[0])

    def from_high(source):
        rows = pl.ds(0, BLK)
        return pltpu.make_async_copy(source.at[slot, :, rows], out.at[:, pl.ds(BLK, BLK)], sems.at[1])

    if own_pair:

        @pl.when(x_at == 0)
        def _():
            from_low(lows[1]).start()

        @pl.when(x_at != 0)
        def _():
            from_low(lows[0]).start()

        @pl.when(x_at == XN - 1)
        def _():
            from_high(highs[1]).start()

        @pl.when(x_at != XN - 1)
        def _():
            from_high(highs[0]).start()

    else:
        from_low(lows[0]).start()
        from_high(highs[0]).start()
    from_low(lows[0]).wait()
    from_high(highs[0]).wait()


def corner(own_pair, place, lows, highs):
    shape = lows[0].shape
    return pl.pallas_call(
        functools.partial(corner_kernel, own_pair),
        in_specs=[SMEM] + [ANY] * (len(lows) + len(highs)),
        out_specs=VMEM,
        out_shape=jax.ShapeDtypeStruct((2, 2 * BLK, shape[3]), jnp.bfloat16),
        scratch_shapes=[pltpu.SemaphoreType.DMA((2,))],
        compiler_params=pltpu.CompilerParams(vmem_limit_bytes=4 * 2**20),
    )(place, *lows, *highs)


def head_scores(query, keys, bias):
    scores = jnp.concatenate(
        [
            lax.dot_general(query, k, (((1,), (1,)), ((), ())), preferred_element_type=jnp.float32)
            for k in keys
        ],
        axis=1,
    )
    return jnp.concatenate([scores[:BLK] + bias[0:1], scores[BLK:] + bias[1:2]], axis=0)


def weighted(weights, values):
    rounded = weights.astype(jnp.bfloat16)
    start, out = 0, 0
    for v in values:
        out = out + jnp.dot(
            rounded[:, start : start + v.shape[0]], v, preferred_element_type=jnp.float32
        )
        start += v.shape[0]
    return out


def own_kernel(
    at_ref, bias_ref, got0, got1, got2, got3, own, oth, z_own, z_oth,
    out_ref, top_ref, sum_ref, keys, values, queries,
):
    me = at_ref[0]
    upper = me >= 2

    def one_head(head, carry):
        lanes = pl.ds(pl.multiple_of(head * HDIM, HDIM), HDIM)
        for slot, got in enumerate((got0, got1, got2, got3)):
            queries[me ^ slot] = got[2, :, lanes]
        for which, store in ((0, keys), (1, values)):
            for slot in range(2):
                store[2 + (me ^ slot)] = own[slot, which, :, lanes]
                store[2 + (me ^ slot ^ 2)] = oth[slot, which, :, lanes]
                at = jnp.where(upper, (me ^ slot) - 2, 6 + (me ^ slot))
                store[at] = z_own[slot, which, :, lanes]
                at = jnp.where(upper, 6 + (me ^ slot ^ 2), (me ^ slot ^ 2) - 2)
                store[at] = z_oth[slot, which, :, lanes]
        for frame in range(GROUP):
            near = [frame + 2 + step for step in FRAME_STEPS]
            scores = head_scores(
                queries[frame], [keys[at] for at in near], bias_ref[frame, :, :OWN_KEYS]
            )
            top = jnp.max(scores, axis=1, keepdims=True)
            weights = jnp.exp2((scores - top) * SCALE)
            total = jnp.sum(weights, axis=1, keepdims=True)
            out_ref[frame, :, lanes] = weighted(weights, [values[at] for at in near])
            top_ref[frame, :, lanes] = jnp.broadcast_to(top, (top.shape[0], HDIM))
            sum_ref[frame, :, lanes] = jnp.broadcast_to(total, (top.shape[0], HDIM))
        return carry

    lax.fori_loop(0, own.shape[3] // HDIM, one_head, 0)


def halo_kernel(
    frames, at_ref, bias_ref, got0, got1, got2, got3, sofar, top_in, sum_in,
    low_own, low_own2, low_oth, high_own, high_own2, high_oth, *rest
):
    corners, (out_ref, keys, values, queries) = rest[:-4], rest[-4:]
    me, x_at = at_ref[0], at_ref[1]
    upper = me >= 2
    length = low_own.shape[2]

    def one_head(head, carry):
        lanes = pl.ds(pl.multiple_of(head * HDIM, HDIM), HDIM)
        below, above = slice(0, length), slice(length, 2 * length)
        for slot, got in enumerate((got0, got1, got2, got3)):
            queries[me ^ slot] = got[2, :, lanes]
        for which, store in ((0, keys), (1, values)):
            for slot in range(2):
                at = 1 + (me ^ slot)
                store[at, below] = jnp.where(
                    x_at == 0, low_own2[slot, which, :, lanes], low_own[slot, which, :, lanes]
                )
                store[at, above] = jnp.where(
                    x_at == XN - 1, high_own2[slot, which, :, lanes], high_own[slot, which, :, lanes]
                )
                at = 1 + (me ^ slot ^ 2)
                store[at, below] = low_oth[slot, which, :, lanes]
                store[at, above] = high_oth[slot, which, :, lanes]
            for arrived, at in zip(corners, (jnp.where(upper, 0, 5), jnp.where(upper, 5, 0))):
                store[at, length - BLK : length + BLK] = arrived[which, :, lanes]
        for at_out, frame in enumerate(frames):
            spans = []
            for step in HALO_STEPS:
                reach = (REACH - abs(step)) * BLK
                spans.append((frame + 1 + step, slice(length - reach, length + reach)))
            scores = head_scores(
                queries[frame], [keys[at, span] for at, span in spans], bias_ref[frame, :, OWN_KEYS:]
            )
            top_own = top_in[frame, :, lanes]
            top = jnp.maximum(top_own, jnp.max(scores, axis=1, keepdims=True))
            again = jnp.exp2((top_own - top) * SCALE)
            weights = jnp.exp2((scores - top[:, 0:1]) * SCALE)
            total = sum_in[frame, :, lanes] * again + jnp.sum(weights, axis=1, keepdims=True)
            out = sofar[frame, :, lanes] * again + weighted(
                weights, [values[at, span] for at, span in spans]
            )
            out_ref[at_out, :, lanes] = (out / total).astype(jnp.bfloat16)
        return carry

    lax.fori_loop(0, low_own.shape[3] // HDIM, one_head, 0)


def attend(kernel, out_shape, scratch, work, place, bias, arrays):
    length, width = arrays[0].shape[1:]
    return pl.pallas_call(
        kernel,
        in_specs=[SMEM] + [VMEM] * (1 + len(arrays)),
        out_specs=jax.tree.map(lambda _: VMEM, out_shape),
        out_shape=out_shape,
        scratch_shapes=[pltpu.VMEM(scratch, jnp.bfloat16)] * 2
        + [pltpu.VMEM((GROUP, length, HDIM), jnp.bfloat16)],
        compiler_params=pltpu.CompilerParams(vmem_limit_bytes=16 * 2**20),
        cost_estimate=pl.CostEstimate(
            flops=4 * work * width * length, bytes_accessed=8_000_000,
            transcendentals=work * width * length // HDIM,
        ),
    )(place, bias, *arrays)


def shards(frame_total, row_total, queries, key_states, value_states, radial_mask):
    length, width = queries.shape[1:]
    part = width // GROUP
    frame_at = lax.axis_index("frame")
    row_at = lax.axis_index("row")
    me = frame_at % GROUP
    x_at = row_at % XN
    place = jnp.stack([me, x_at]).astype(jnp.int32)

    def send(array, target):
        return lax.ppermute(array, AXES, pairs_of(frame_total, row_total, target))

    packed = pl.pallas_call(
        pack_kernel,
        in_specs=[SMEM] + [ANY] * 3,
        out_specs=[VMEM] * GROUP,
        out_shape=[jax.ShapeDtypeStruct((3, length, part), jnp.bfloat16)] * GROUP,
        scratch_shapes=[pltpu.SemaphoreType.DMA((GROUP, 3))],
        compiler_params=pltpu.CompilerParams(vmem_limit_bytes=56 * 2**20),
    )(place, queries[0], key_states[0], value_states[0])

    def flip(bits):
        return lambda f, r: (f ^ bits, r)

    groups = [list(range(f, f + GROUP)) for f in range(0, frame_total, GROUP)]
    arrived = [packed[0]] + [send(packed[s], flip(s)) for s in range(1, GROUP)]
    own = jnp.stack([arrived[0][:2], arrived[1][:2]])
    oth = jnp.stack([arrived[2][:2], arrived[3][:2]])

    def row_first(by):
        edge = XN - 1 if by > 0 else 0
        return lambda f, r: (f, r + by) if r % XN != edge else (f, r - by * (XN - 1))

    def row_second(by):
        edge = 0 if by > 0 else XN - 1
        return lambda f, r: (f, r + by * XN) if r % XN == edge else None

    def row_direct(by):
        return lambda f, r: (f, r + by)

    def z_target(own_pair):
        def target(f, r):
            up = (f % GROUP >= 2) == own_pair
            return (f + GROUP if up else f - GROUP, r)

        return target

    low_own, high_own = send(own, row_first(1)), send(own, row_first(-1))
    z_own = send(own, z_target(True))
    low_own2, high_own2 = send(low_own, row_second(1)), send(high_own, row_second(-1))
    low_oth, high_oth = send(oth, row_direct(1)), send(oth, row_direct(-1))
    later, z_own, low_own, high_own = lax.optimization_barrier((oth, z_own, low_own, high_own))
    z_oth = send(later, z_target(False))
    bias = bias_of(radial_mask, frame_at - me, row_at, frame_total)
    sums = [jax.ShapeDtypeStruct((GROUP, length, part), jnp.float32)] * 3
    partial = attend(
        own_kernel, sums, (GROUP + 4, length, HDIM), GROUP * OWN_KEYS, place, bias,
        arrived + [own, oth, z_own, z_oth],
    )
    partial, low_own2, high_own2, low_oth, high_oth = lax.optimization_barrier(
        (partial, low_own2, high_own2, low_oth, high_oth)
    )
    c_own = corner(True, place, [low_own, low_own2], [high_own, high_own2])
    c_own, low_oth, high_oth = lax.optimization_barrier((c_own, low_oth, high_oth))
    c_oth = corner(False, place, [low_oth], [high_oth])
    c_own, c_oth = send(c_own, z_target(True)), send(c_oth, z_target(False))

    arrays = arrived + list(partial) + [low_own, low_own2, low_oth, high_own, high_own2, high_oth]
    half = jax.ShapeDtypeStruct((2, length, part), jnp.bfloat16)
    halo_keys = bias.shape[2] - OWN_KEYS
    middle, edge = [
        attend(
            functools.partial(halo_kernel, frames), half, (GROUP + 2, 2 * length, HDIM),
            2 * halo_keys, place, bias, arrays + corners,
        )
        for frames, corners in (((1, 2), []), ((0, 3), [c_own, c_oth]))
    ]
    by_frame = jnp.stack([edge[0], middle[0], middle[1], edge[1]])
    back = lax.all_to_all(by_frame, "frame", 0, 0, axis_index_groups=groups)
    result = pl.pallas_call(
        unpack_kernel,
        in_specs=[ANY],
        out_specs=ANY,
        out_shape=jax.ShapeDtypeStruct((length, width), jnp.bfloat16),
        scratch_shapes=[pltpu.SemaphoreType.DMA((GROUP,))],
        compiler_params=pltpu.CompilerParams(vmem_limit_bytes=4 * 2**20),
    )(back)
    return result[None]


def solution(mesh):
    sharded = P("frame", "row", None)
    body = functools.partial(shards, mesh.shape["frame"], mesh.shape["row"])
    return jax.shard_map(
        body, mesh=mesh, in_specs=(sharded, sharded, sharded, P()), out_specs=sharded, check_vma=False
    )
```

time: 196 us -> 120 us (0.61)
  the two profiles are of different devices: /device:TPU:223 before, /device:TPU:240 now
where the time goes in v1:
time: 120 us; the launch traced here: 119 us
  starting transfers between devices  40.7 us (34%)
  Pallas kernels  30.2 us (25%)
  waiting for transfers between devices  28 us (23%)
  blocking collectives  12.7 us (11%)
  local copies, waits for them, and re-layouts  4.73 us (4%)
  other arithmetic  1.9 us (2%)
    ppermute x13, starting transfers between devices, send(): return lax.ppermute(array, AXES, pairs_of(frame_total, row_total, target))  40.7 us
    ppermute x13, waiting for transfers between devices, send(): return lax.ppermute(array, AXES, pairs_of(frame_total, row_total, target))  28 us
    pallas_call x3, Pallas kernels, attend(): pl.pallas_call(kernel, in_specs=[SMEM] + [VMEM] * (1 + len(arrays)), out_...  23.3 us
    all_to_all x1, blocking collectives, shards(): back = lax.all_to_all(by_frame, 'frame', 0, 0, axis_index_groups=groups)  12.7 us
    pallas_call x1, Pallas kernels, shards(): pl.pallas_call(pack_kernel, in_specs=[SMEM] + [ANY] * 3, out_specs=[VMEM]...  3.64 us
    unnamed x21, local copies, waits for them, and re-layouts  3.17 us
  transfers between devices with their start and end apart: 13, of which 4 were waited for; matrix products, arithmetic and copies ran while one was open for 2% of the time, Pallas kernels for 15%

profile of v1, /device:TPU:240, one launch (start us, length us, event | category | flops | bytes accessed | tf_op | source)
XLA Modules:
  0.0 118.5 jit_solution(14877856514469153648)
XLA Ops:
  0.0 0.6 pad_add_fusion.at_ref
  0.6 3.6 %shard_map.73 = (bf16[3,128,640]{2,1,0:T(8,128)(2,1)}, bf16[3,128,640]{2,1,0:T(8,128)(2,1)}, bf16[3,128,640]{2,1,0:T(8,128)(2,1)}, bf16[3,128,640]{2,1,0:T(8,128)(2,1)}) custom-call(s32[2]{0:T(128)} %pad_add_fusion.at_ref, bf16[128,2560]{1,0:T(8,128)(2,1)} %bitcast.14, bf16[128,2560]{1,0:T(8,128)(2,1)} %bitcast.15, bf16[128,2560]{1,0:T(8,128)(2,1)} %bitcast.16), custom_call_target="tpu_custom_call" | custom-call | tf_op jit(solution)/shard_map/pallas_call | solution.py:292
  4.3 1.9 %collective-permute-start = (bf16[3,128,640]{2,1,0:T(8,128)(2,1)}, bf16[3,128,640]{2,1,0:T(8,128)(2,1)S(1)}, u32[]{:S(2)}, u32[]{:S(2)}) collective-permute-start(bf16[3,128,640]{2,1,0:T(8,128)(2,1)} %get-tuple-element.27), channel_id=1, source_target_pairs={{0,16},{1,17},{2,18},{3,19},{4,20},{5,21},{6,22},{7,23},{8,24},{9,... | collective-permute-start | bytes 1474568 | tf_op jit(solution)/shard_map/ppermute | solution.py:290
  6.2 2.6 %collective-permute-start.1 = (bf16[3,128,640]{2,1,0:T(8,128)(2,1)}, bf16[3,128,640]{2,1,0:T(8,128)(2,1)S(1)}, u32[]{:S(2)}, u32[]{:S(2)}) collective-permute-start(bf16[3,128,640]{2,1,0:T(8,128)(2,1)} %get-tuple-element.28), channel_id=1, source_target_pairs={{0,32},{1,33},{2,34},{3,35},{4,36},{5,37},{6,38},{7,39},{8,40},{9,... | collective-permute-start | bytes 1474568 | tf_op jit(solution)/shard_map/ppermute | solution.py:290
  8.8 3.1 %collective-permute-start.2 = (bf16[3,128,640]{2,1,0:T(8,128)(2,1)}, bf16[3,128,640]{2,1,0:T(8,128)(2,1)S(1)}, u32[]{:S(2)}, u32[]{:S(2)}) collective-permute-start(bf16[3,128,640]{2,1,0:T(8,128)(2,1)} %get-tuple-element.29), channel_id=1, source_target_pairs={{0,48},{1,49},{2,50},{3,51},{4,52},{5,53},{6,54},{7,55},{8,56},{9,... | collective-permute-start | bytes 1474568 | tf_op jit(solution)/shard_map/ppermute | solution.py:290
  12.0 0.1 copy.15
  12.4 1.0 slice_bitcast_fusion.3
  13.5 1.9 %collective-permute-start.3 = (bf16[2,2,128,640]{3,2,1,0:T(8,128)(2,1)S(1)}, bf16[2,2,128,640]{3,2,1,0:T(8,128)(2,1)S(1)}, u32[]{:S(2)}, u32[]{:S(2)}) collective-permute-start(bf16[2,2,128,640]{3,2,1,0:T(8,128)(2,1)S(1)} %pad_maximum_fusion.own), channel_id=1, source_target_pairs={{32,96},{33,97},{34,98},{35,99},{36,100},{37,101},{38,102},{39,103... | collective-permute-start | bytes 1966088 | tf_op jit(solution)/shard_map/ppermute | solution.py:290
  15.5 3.4 %collective-permute-start.4 = (bf16[2,2,128,640]{3,2,1,0:T(8,128)(2,1)S(1)}, bf16[2,2,128,640]{3,2,1,0:T(8,128)(2,1)}, u32[]{:S(2)}, u32[]{:S(2)}) collective-permute-start(bf16[2,2,128,640]{3,2,1,0:T(8,128)(2,1)S(1)} %pad_maximum_fusion.own), channel_id=1, source_target_pairs={{0,1},{1,2},{2,3},{3,0},{4,5},{5,6},{6,7},{7,4},{8,9},{9,10},{10,1... | collective-permute-start | bytes 1966088 | tf_op jit(solution)/shard_map/ppermute | solution.py:290
  18.9 3.7 %collective-permute-start.5 = (bf16[2,2,128,640]{3,2,1,0:T(8,128)(2,1)S(1)}, bf16[2,2,128,640]{3,2,1,0:T(8,128)(2,1)}, u32[]{:S(2)}, u32[]{:S(2)}) collective-permute-start(bf16[2,2,128,640]{3,2,1,0:T(8,128)(2,1)S(1)} %pad_maximum_fusion.own), channel_id=1, source_target_pairs={{0,3},{1,0},{2,1},{3,2},{4,7},{5,4},{6,5},{7,6},{8,11},{9,8},{10,9... | collective-permute-start | bytes 1966088 | tf_op jit(solution)/shard_map/ppermute | solution.py:290
  22.6 9.5 %collective-permute-done.2.got3 = bf16[3,128,640]{2,1,0:T(8,128)(2,1)S(1)} collective-permute-done((bf16[3,128,640]{2,1,0:T(8,128)(2,1)}, bf16[3,128,640]{2,1,0:T(8,128)(2,1)S(1)}, u32[]{:S(2)}, u32[]{:S(2)}) %collective-permute-start.2) | collective-permute-done | bytes 491552 | tf_op jit(solution)/shard_map/ppermute | solution.py:290
  32.1 0.9 pad_maximum_fusion.1.oth
  33.1 3.4 %collective-permute-start.9 = (bf16[2,2,128,640]{3,2,1,0:T(8,128)(2,1)}, bf16[2,2,128,640]{3,2,1,0:T(8,128)(2,1)S(1)}, u32[]{:S(2)}, u32[]{:S(2)}) collective-permute-start(bf16[2,2,128,640]{3,2,1,0:T(8,128)(2,1)} %pad_maximum_fusion.1.oth), channel_id=1, source_target_pairs={{0,1},{1,2},{2,3},{3,4},{4,5},{5,6},{6,7},{7,8},{8,9},{9,10},{10,1... | collective-permute-start | bytes 1966088 | tf_op jit(solution)/shard_map/ppermute | solution.py:290
  36.5 5.5 %collective-permute-start.10 = (bf16[2,2,128,640]{3,2,1,0:T(8,128)(2,1)}, bf16[2,2,128,640]{3,2,1,0:T(8,128)(2,1)S(1)}, u32[]{:S(2)}, u32[]{:S(2)}) collective-permute-start(bf16[2,2,128,640]{3,2,1,0:T(8,128)(2,1)} %pad_maximum_fusion.1.oth), channel_id=1, source_target_pairs={{1,0},{2,1},{3,2},{4,3},{5,4},{6,5},{7,6},{8,7},{9,8},{10,9},{11,1... | collective-permute-start | bytes 1966088 | tf_op jit(solution)/shard_map/ppermute | solution.py:290
  41.9 0.8 copy-done.4
  42.8 5.5 %collective-permute-start.6 = (bf16[2,2,128,640]{3,2,1,0:T(8,128)(2,1)}, bf16[2,2,128,640]{3,2,1,0:T(8,128)(2,1)}, u32[]{:S(2)}, u32[]{:S(2)}) collective-permute-start(bf16[2,2,128,640]{3,2,1,0:T(8,128)(2,1)} %pad_maximum_fusion.1.oth), channel_id=1, source_target_pairs={{0,64},{1,65},{2,66},{3,67},{4,68},{5,69},{6,70},{7,71},{8,72},{9,... | collective-permute-start | bytes 1966088 | tf_op jit(solution)/shard_map/ppermute | solution.py:290
  48.3 1.3 %collective-permute-start.7 = (bf16[2,2,128,640]{3,2,1,0:T(8,128)(2,1)}, bf16[2,2,128,640]{3,2,1,0:T(8,128)(2,1)}, u32[]{:S(2)}, u32[]{:S(2)}) collective-permute-start(bf16[2,2,128,640]{3,2,1,0:T(8,128)(2,1)} %collective-permute-done.4.refs_0_.low_own), channel_id=1, source_target_pairs={{0,4},{4,8},{8,12},{16,20},{20,24},{24,28},{32,36},{36,40},{40,44}... | collective-permute-start | bytes 1966088 | tf_op jit(solution)/shard_map/ppermute | solution.py:290
  49.6 1.5 %collective-permute-start.8 = (bf16[2,2,128,640]{3,2,1,0:T(8,128)(2,1)}, bf16[2,2,128,640]{3,2,1,0:T(8,128)(2,1)}, u32[]{:S(2)}, u32[]{:S(2)}) collective-permute-start(bf16[2,2,128,640]{3,2,1,0:T(8,128)(2,1)} %collective-permute-done.5.refs_2_.high_own), channel_id=1, source_target_pairs={{7,3},{11,7},{15,11},{23,19},{27,23},{31,27},{39,35},{43,39},{47,4... | collective-permute-start | bytes 1966088 | tf_op jit(solution)/shard_map/ppermute | solution.py:290
  51.4 11.4 %collective-permute-done.6.z_oth = bf16[2,2,128,640]{3,2,1,0:T(8,128)(2,1)} collective-permute-done((bf16[2,2,128,640]{3,2,1,0:T(8,128)(2,1)}, bf16[2,2,128,640]{3,2,1,0:T(8,128)(2,1)}, u32[]{:S(2)}, u32[]{:S(2)}) %collective-permute-start.6) | collective-permute-done | bytes 655392 | tf_op jit(solution)/shard_map/ppermute | solution.py:290
  62.8 1.1 copy-done.3
  63.9 1.1 copy-done.5
  64.9 9.9 %shard_map.74 = (f32[4,128,640]{2,1,0:T(8,128)S(1)}, f32[4,128,640]{2,1,0:T(8,128)S(1)}, f32[4,128,640]{2,1,0:T(8,128)S(1)}) custom-call(s32[2]{0:T(128)S(1)} %copy-done.6, f32[4,2,1152]{2,1,0:T(2,128)S(1)} %reshape.59.bias_ref, bf16[3,128,640]{2,1,0:T(8,128)(2,1)S(1)} %copy-done.1, bf16[3,128,640]{2,1,0:T(8,128)(2,1)S(1)} %collective-permute-done.got1, ...), custom_call_target="tpu_custom_call" | custom-call | flops 838860800 | bytes 8000000 | tf_op jit(solution)/shard_map/pallas_call | solution.py:265
  74.9 6.9 %collective-permute-done.7.refs_1_.low_own2 = bf16[2,2,128,640]{3,2,1,0:T(8,128)(2,1)} collective-permute-done((bf16[2,2,128,640]{3,2,1,0:T(8,128)(2,1)}, bf16[2,2,128,640]{3,2,1,0:T(8,128)(2,1)}, u32[]{:S(2)}, u32[]{:S(2)}) %collective-permute-start.7) | collective-permute-done | bytes 655392 | tf_op jit(solution)/shard_map/ppermute | solution.py:290
  81.8 1.6 %shard_map.75 = bf16[2,128,640]{2,1,0:T(8,128)(2,1)S(1)} custom-call(s32[2]{0:T(128)S(1)} %copy-done.6, bf16[2,2,128,640]{3,2,1,0:T(8,128)(2,1)} %collective-permute-done.4.refs_0_.low_own, bf16[2,2,128,640]{3,2,1,0:T(8,128)(2,1)} %collective-permute-done.7.refs_1_.low_own2, bf16[2,2,128,640]{3,2,1,0:T(8,128)(2,1)} %collective-permute-done.5.refs_2_.high_own, ...), custom_call_target="tpu_custom_call" | custom-call | tf_op jit(solution)/shard_map/pallas_call | solution.py:146
  83.4 1.9 %collective-permute-start.11 = (bf16[2,128,640]{2,1,0:T(8,128)(2,1)S(1)}, bf16[2,128,640]{2,1,0:T(8,128)(2,1)S(1)}, u32[]{:S(2)}, u32[]{:S(2)}) collective-permute-start(bf16[2,128,640]{2,1,0:T(8,128)(2,1)S(1)} %shard_map.75), channel_id=1, source_target_pairs={{32,96},{33,97},{34,98},{35,99},{36,100},{37,101},{38,102},{39,103... | collective-permute-start | bytes 983048 | tf_op jit(solution)/shard_map/ppermute | solution.py:290
  85.3 0.8 shard_map.76
  86.1 5.1 %collective-permute-start.12 = (bf16[2,128,640]{2,1,0:T(8,128)(2,1)S(1)}, bf16[2,128,640]{2,1,0:T(8,128)(2,1)S(1)}, u32[]{:S(2)}, u32[]{:S(2)}) collective-permute-start(bf16[2,128,640]{2,1,0:T(8,128)(2,1)S(1)} %shard_map.76), channel_id=1, source_target_pairs={{0,64},{1,65},{2,66},{3,67},{4,68},{5,69},{6,70},{7,71},{8,72},{9,... | collective-permute-start | bytes 983048 | tf_op jit(solution)/shard_map/ppermute | solution.py:290
  91.2 6.6 %shard_map.78 = bf16[2,128,640]{2,1,0:T(8,128)(2,1)S(1)} custom-call(s32[2]{0:T(128)S(1)} %copy-done.6, f32[4,2,1152]{2,1,0:T(2,128)S(1)} %reshape.59.bias_ref, bf16[3,128,640]{2,1,0:T(8,128)(2,1)S(1)} %copy-done.1, bf16[3,128,640]{2,1,0:T(8,128)(2,1)S(1)} %collective-permute-done.got1, bf16[3,128,640]{2,1,0:T(8,128)(2,1)S(1)} %collective-permute-done.1.got2, ...), custom_call_target="tpu_custom_call" | custom-call | flops 335544320 | bytes 8000000 | tf_op jit(solution)/shard_map/pallas_call | solution.py:265
  97.9 0.2 collective-permute-done.12.rest_1_
  98.1 6.8 %shard_map.77 = bf16[2,128,640]{2,1,0:T(8,128)(2,1)S(1)} custom-call(s32[2]{0:T(128)S(1)} %copy-done.6, f32[4,2,1152]{2,1,0:T(2,128)S(1)} %reshape.59.bias_ref, bf16[3,128,640]{2,1,0:T(8,128)(2,1)S(1)} %copy-done.1, bf16[3,128,640]{2,1,0:T(8,128)(2,1)S(1)} %collective-permute-done.got1, bf16[3,128,640]{2,1,0:T(8,128)(2,1)S(1)} %collective-permute-done.1.got2, ...), custom_call_target="tpu_custom_call" | custom-call | flops 335544320 | bytes 8000000 | tf_op jit(solution)/shard_map/pallas_call | solution.py:265
  105.0 12.7 %all_to_all.5.in_ref = bf16[4,128,640]{2,1,0:T(8,128)(2,1)S(1)} all-to-all(bf16[4,128,640]{2,1,0:T(8,128)(2,1)S(1)} %pad_maximum_fusion.2), channel_id=1, replica_groups={{0,16,32,48},{64,80,96,112},{128,144,160,176},{192,208,224,240},{256,27..., dimensions={0} | all-to-all | bytes 1310720 | tf_op jit(solution)/shard_map/all_to_all | solution.py:358
  117.7 0.9 shard_map.79
  (45 shorter events, 1.0 us)
Async XLA Ops:
  0.0 11.9 %copy-start = (s32[5,32,5]{1,2,0:T(8,128)S(1)}, s32[5,32,5]{1,2,0:T(8,128)}, u32[]{:S(2)}) copy-start(s32[5,32,5]{1,2,0:T(8,128)} %param.10) | copy-start | bytes 9604
  0.0 12.2 %copy-start.7 = (f32[2,18,50]{2,0,1:T(2,128)S(1)}, f32[2,18,50]{2,0,1:T(2,128)}, u32[]{:S(2)}) copy-start(f32[2,18,50]{2,0,1:T(2,128)} %constant.46.clone) | copy-start | bytes 21604
  4.3 9.1 %collective-permute-start = (bf16[3,128,640]{2,1,0:T(8,128)(2,1)}, bf16[3,128,640]{2,1,0:T(8,128)(2,1)S(1)}, u32[]{:S(2)}, u32[]{:S(2)}) collective-permute-start(bf16[3,128,640]{2,1,0:T(8,128)(2,1)} %get-tuple-element.27), channel_id=1, source_target_pairs={{0,16},{1,17},{2,18},{3,19},{4,20},{5,21},{6,22},{7,23},{8,24},{9,... | collective-permute-start | bytes 1474568 | tf_op jit(solution)/shard_map/ppermute | solution.py:290
  6.2 25.9 %collective-permute-start.1 = (bf16[3,128,640]{2,1,0:T(8,128)(2,1)}, bf16[3,128,640]{2,1,0:T(8,128)(2,1)S(1)}, u32[]{:S(2)}, u32[]{:S(2)}) collective-permute-start(bf16[3,128,640]{2,1,0:T(8,128)(2,1)} %get-tuple-element.28), channel_id=1, source_target_pairs={{0,32},{1,33},{2,34},{3,35},{4,36},{5,37},{6,38},{7,39},{8,40},{9,... | collective-permute-start | bytes 1474568 | tf_op jit(solution)/shard_map/ppermute | solution.py:290
  8.8 23.3 %collective-permute-start.2 = (bf16[3,128,640]{2,1,0:T(8,128)(2,1)}, bf16[3,128,640]{2,1,0:T(8,128)(2,1)S(1)}, u32[]{:S(2)}, u32[]{:S(2)}) collective-permute-start(bf16[3,128,640]{2,1,0:T(8,128)(2,1)} %get-tuple-element.29), channel_id=1, source_target_pairs={{0,48},{1,49},{2,50},{3,51},{4,52},{5,53},{6,54},{7,55},{8,56},{9,... | collective-permute-start | bytes 1474568 | tf_op jit(solution)/shard_map/ppermute | solution.py:290
  13.5 19.5 %copy-start.2 = (bf16[2,2,128,640]{3,2,1,0:T(8,128)(2,1)}, bf16[2,2,128,640]{3,2,1,0:T(8,128)(2,1)S(1)}, u32[]{:S(2)}) copy-start(bf16[2,2,128,640]{3,2,1,0:T(8,128)(2,1)S(1)} %pad_maximum_fusion.own) | copy-start | bytes 1966084
  13.5 28.4 %collective-permute-start.3 = (bf16[2,2,128,640]{3,2,1,0:T(8,128)(2,1)S(1)}, bf16[2,2,128,640]{3,2,1,0:T(8,128)(2,1)S(1)}, u32[]{:S(2)}, u32[]{:S(2)}) collective-permute-start(bf16[2,2,128,640]{3,2,1,0:T(8,128)(2,1)S(1)} %pad_maximum_fusion.own), channel_id=1, source_target_pairs={{32,96},{33,97},{34,98},{35,99},{36,100},{37,101},{38,102},{39,103... | collective-permute-start | bytes 1966088 | tf_op jit(solution)/shard_map/ppermute | solution.py:290
  15.5 27.3 %collective-permute-start.4 = (bf16[2,2,128,640]{3,2,1,0:T(8,128)(2,1)S(1)}, bf16[2,2,128,640]{3,2,1,0:T(8,128)(2,1)}, u32[]{:S(2)}, u32[]{:S(2)}) collective-permute-start(bf16[2,2,128,640]{3,2,1,0:T(8,128)(2,1)S(1)} %pad_maximum_fusion.own), channel_id=1, source_target_pairs={{0,1},{1,2},{2,3},{3,0},{4,5},{5,6},{6,7},{7,4},{8,9},{9,10},{10,1... | collective-permute-start | bytes 1966088 | tf_op jit(solution)/shard_map/ppermute | solution.py:290
  18.9 23.9 %collective-permute-start.5 = (bf16[2,2,128,640]{3,2,1,0:T(8,128)(2,1)S(1)}, bf16[2,2,128,640]{3,2,1,0:T(8,128)(2,1)}, u32[]{:S(2)}, u32[]{:S(2)}) collective-permute-start(bf16[2,2,128,640]{3,2,1,0:T(8,128)(2,1)S(1)} %pad_maximum_fusion.own), channel_id=1, source_target_pairs={{0,3},{1,0},{2,1},{3,2},{4,7},{5,4},{6,5},{7,6},{8,11},{9,8},{10,9... | collective-permute-start | bytes 1966088 | tf_op jit(solution)/shard_map/ppermute | solution.py:290
  22.6 28.5 %copy-start.9 = (s32[18]{0:T(128)S(1)}, s32[18]{0:T(128)}, u32[]{:S(2)}) copy-start(s32[18]{0:T(128)} %constant.48.clone) | copy-start | bytes 220
  22.6 28.5 %copy-start.8 = (s32[18]{0:T(128)S(1)}, s32[18]{0:T(128)}, u32[]{:S(2)}) copy-start(s32[18]{0:T(128)} %constant.47.clone) | copy-start | bytes 220
  22.6 40.2 %copy-start.1 = (bf16[3,128,640]{2,1,0:T(8,128)(2,1)S(1)}, bf16[3,128,640]{2,1,0:T(8,128)(2,1)}, u32[]{:S(2)}) copy-start(bf16[3,128,640]{2,1,0:T(8,128)(2,1)} %get-tuple-element.26.got0) | copy-start | bytes 1474564
  22.6 40.2 %copy-start.6 = (s32[2]{0:T(128)S(1)}, s32[2]{0:T(128)}, u32[]{:S(2)}) copy-start(s32[2]{0:T(128)} %pad_add_fusion.at_ref) | copy-start | bytes 28
  33.1 41.8 %collective-permute-start.9 = (bf16[2,2,128,640]{3,2,1,0:T(8,128)(2,1)}, bf16[2,2,128,640]{3,2,1,0:T(8,128)(2,1)S(1)}, u32[]{:S(2)}, u32[]{:S(2)}) collective-permute-start(bf16[2,2,128,640]{3,2,1,0:T(8,128)(2,1)} %pad_maximum_fusion.1.oth), channel_id=1, source_target_pairs={{0,1},{1,2},{2,3},{3,4},{4,5},{5,6},{6,7},{7,8},{8,9},{9,10},{10,1... | collective-permute-start | bytes 1966088 | tf_op jit(solution)/shard_map/ppermute | solution.py:290
  36.5 38.4 %collective-permute-start.10 = (bf16[2,2,128,640]{3,2,1,0:T(8,128)(2,1)}, bf16[2,2,128,640]{3,2,1,0:T(8,128)(2,1)S(1)}, u32[]{:S(2)}, u32[]{:S(2)}) collective-permute-start(bf16[2,2,128,640]{3,2,1,0:T(8,128)(2,1)} %pad_maximum_fusion.1.oth), channel_id=1, source_target_pairs={{1,0},{2,1},{3,2},{4,3},{5,4},{6,5},{7,6},{8,7},{9,8},{10,9},{11,1... | collective-permute-start | bytes 1966088 | tf_op jit(solution)/shard_map/ppermute | solution.py:290
  41.9 0.8 copy-start.4
  42.8 20.0 %collective-permute-start.6 = (bf16[2,2,128,640]{3,2,1,0:T(8,128)(2,1)}, bf16[2,2,128,640]{3,2,1,0:T(8,128)(2,1)}, u32[]{:S(2)}, u32[]{:S(2)}) collective-permute-start(bf16[2,2,128,640]{3,2,1,0:T(8,128)(2,1)} %pad_maximum_fusion.1.oth), channel_id=1, source_target_pairs={{0,64},{1,65},{2,66},{3,67},{4,68},{5,69},{6,70},{7,71},{8,72},{9,... | collective-permute-start | bytes 1966088 | tf_op jit(solution)/shard_map/ppermute | solution.py:290
  48.3 33.5 %collective-permute-start.7 = (bf16[2,2,128,640]{3,2,1,0:T(8,128)(2,1)}, bf16[2,2,128,640]{3,2,1,0:T(8,128)(2,1)}, u32[]{:S(2)}, u32[]{:S(2)}) collective-permute-start(bf16[2,2,128,640]{3,2,1,0:T(8,128)(2,1)} %collective-permute-done.4.refs_0_.low_own), channel_id=1, source_target_pairs={{0,4},{4,8},{8,12},{16,20},{20,24},{24,28},{32,36},{36,40},{40,44}... | collective-permute-start | bytes 1966088 | tf_op jit(solution)/shard_map/ppermute | solution.py:290
  49.6 32.2 %collective-permute-start.8 = (bf16[2,2,128,640]{3,2,1,0:T(8,128)(2,1)}, bf16[2,2,128,640]{3,2,1,0:T(8,128)(2,1)}, u32[]{:S(2)}, u32[]{:S(2)}) collective-permute-start(bf16[2,2,128,640]{3,2,1,0:T(8,128)(2,1)} %collective-permute-done.5.refs_2_.high_own), channel_id=1, source_target_pairs={{7,3},{11,7},{15,11},{23,19},{27,23},{31,27},{39,35},{43,39},{47,4... | collective-permute-start | bytes 1966088 | tf_op jit(solution)/shard_map/ppermute | solution.py:290
  62.8 1.1 copy-start.3
  63.9 1.1 copy-start.5
  83.4 14.5 %collective-permute-start.11 = (bf16[2,128,640]{2,1,0:T(8,128)(2,1)S(1)}, bf16[2,128,640]{2,1,0:T(8,128)(2,1)S(1)}, u32[]{:S(2)}, u32[]{:S(2)}) collective-permute-start(bf16[2,128,640]{2,1,0:T(8,128)(2,1)S(1)} %shard_map.75), channel_id=1, source_target_pairs={{32,96},{33,97},{34,98},{35,99},{36,100},{37,101},{38,102},{39,103... | collective-permute-start | bytes 983048 | tf_op jit(solution)/shard_map/ppermute | solution.py:290
  86.1 12.0 %collective-permute-start.12 = (bf16[2,128,640]{2,1,0:T(8,128)(2,1)S(1)}, bf16[2,128,640]{2,1,0:T(8,128)(2,1)S(1)}, u32[]{:S(2)}, u32[]{:S(2)}) collective-permute-start(bf16[2,128,640]{2,1,0:T(8,128)(2,1)S(1)} %shard_map.76), channel_id=1, source_target_pairs={{0,64},{1,65},{2,66},{3,67},{4,68},{5,69},{6,70},{7,71},{8,72},{9,... | collective-permute-start | bytes 983048 | tf_op jit(solution)/shard_map/ppermute | solution.py:290

commit v2 on v1

v2 whole, which is shorter than its diff:
```python
import functools

import jax
import jax.numpy as jnp
import numpy as np
from jax import lax
from jax.experimental import pallas as pl
from jax.experimental.pallas import tpu as pltpu
from jax.sharding import PartitionSpec as P

HDIM = 128
BLK = 64
REACH = 2
NEG = -1e30
SCALE = HDIM ** -0.5 * 1.4426950408889634
AXES = ("frame", "row")
GROUP = 4
XN = 4
VMEM = pl.BlockSpec(memory_space=pltpu.VMEM)
SMEM = pl.BlockSpec(memory_space=pltpu.SMEM)
ANY = pl.BlockSpec(memory_space=pl.ANY)
FRAME_STEPS = (-2, -1, 0, 1, 2)
HALO_STEPS = (-1, 0, 1)
OWN_KEYS = 2 * BLK * len(FRAME_STEPS)


def pairs_of(frames, rows, target):
    pairs = []
    for frame in range(frames):
        for row in range(rows):
            to = target(frame, row)
            if to is not None and 0 <= to[0] < frames and 0 <= to[1] < rows:
                pairs.append((frame * rows + row, to[0] * rows + to[1]))
    return pairs


def key_block_table():
    own = [(step, block) for step in FRAME_STEPS for block in (0, 1)]
    halo = []
    for step in HALO_STEPS:
        reach = REACH - abs(step)
        halo += [(step, block) for block in range(-reach, 0)]
        halo += [(step, block) for block in range(2, 2 + reach)]
    return own + halo


def bias_of(radial_mask, frame_first, row_at, frame_total):
    table = key_block_table()
    offsets = 2 * REACH + 1
    pick = np.zeros((2, len(table), offsets * 2 * offsets), np.float32)
    for query in range(2):
        for at, (step, block) in enumerate(table):
            offset = block - query + REACH
            if 0 <= offset < offsets:
                pick[query, at, ((step + REACH) * 2 + query) * offsets + offset] = 1.0
    rows = lax.dynamic_slice_in_dim(radial_mask, row_at * 2, 2, 1)
    chosen = jnp.sum(jnp.asarray(pick) * rows.reshape(1, 1, -1).astype(jnp.float32), axis=2)
    steps = jnp.asarray(np.array([s for s, _ in table], np.int32))
    blocks = jnp.asarray(np.array([b for _, b in table], np.int32)) + row_at * 2
    inside = (blocks >= 0) & (blocks < radial_mask.shape[1])
    frames = frame_first + jnp.arange(GROUP, dtype=jnp.int32)[:, None] + steps[None, :]
    valid = (frames >= 0) & (frames < frame_total) & inside[None, :]
    allowed = (chosen[None] > 0) & valid[:, None, :]
    bias = jnp.where(allowed, 0.0, NEG).astype(jnp.float32)
    return jnp.repeat(bias, BLK, axis=2)


def pack_kernel(at_ref, q_ref, k_ref, v_ref, out0, out1, out2, out3, sems):
    me = at_ref[0]
    outs = (out0, out1, out2, out3)
    width = out0.shape[2]
    copies = []
    for slot in (1, 2, 3, 0):
        columns = pl.ds(pl.multiple_of((me ^ slot) * width, HDIM), width)
        for which, source in enumerate((k_ref, v_ref, q_ref)):
            copies.append(
                pltpu.make_async_copy(
                    source.at[:, columns], outs[slot].at[which], sems.at[slot, which]
                )
            )
    for copy in copies:
        copy.start()
    for copy in copies:
        copy.wait()


def unpack_kernel(in_ref, out_ref, sems):
    width = in_ref.shape[2]
    copies = [
        pltpu.make_async_copy(
            in_ref.at[part], out_ref.at[:, pl.ds(part * width, width)], sems.at[part]
        )
        for part in range(GROUP)
    ]
    for copy in copies:
        copy.start()
    for copy in copies:
        copy.wait()


def join_kernel(first, second, *rest):
    out, sems = rest[-2:]
    copies = [
        pltpu.make_async_copy(source.at[0:2], out.at[slot], sems.at[slot])
        for slot, source in enumerate((first, second))
    ]
    for copy in copies:
        copy.start()
    for copy in copies:
        copy.wait()


def join(first, second, *after):
    return pl.pallas_call(
        join_kernel,
        in_specs=[ANY] * (2 + len(after)),
        out_specs=VMEM,
        out_shape=jax.ShapeDtypeStruct((2, 2) + first.shape[1:], jnp.bfloat16),
        scratch_shapes=[pltpu.SemaphoreType.DMA((2,))],
        compiler_params=pltpu.CompilerParams(vmem_limit_bytes=4 * 2**20),
    )(first, second, *after)


def wrapped_kernel(at_ref, low, high, after, out, sem):
    del after
    x_at = at_ref[1]

    @pl.when(x_at == 0)
    def _():
        pltpu.make_async_copy(low, out, sem).start()

    @pl.when(x_at != 0)
    def _():
        pltpu.make_async_copy(high, out, sem).start()

    pltpu.make_async_copy(low, out, sem).wait()


def wrapped_of(place, low, high, after):
    return pl.pallas_call(
        wrapped_kernel,
        in_specs=[SMEM] + [ANY] * 3,
        out_specs=VMEM,
        out_shape=jax.ShapeDtypeStruct(low.shape, jnp.bfloat16),
        scratch_shapes=[pltpu.SemaphoreType.DMA(())],
        compiler_params=pltpu.CompilerParams(vmem_limit_bytes=4 * 2**20),
    )(place, low, high, after)


def corner_kernel(own_pair, at_ref, *refs):
    me, x_at = at_ref[0], at_ref[1]
    out, sems = refs[-2], refs[-1]
    lows, highs = refs[: (len(refs) - 2) // 2], refs[(len(refs) - 2) // 2 : -2]
    length = lows[0].shape[2]
    if own_pair:
        slot = jnp.where(me < 2, me, 3 - me)
    else:
        slot = jnp.where(me < 2, 1 - me, me - 2)

    def from_low(source):
        rows = pl.ds(length - BLK, BLK)
        return pltpu.make_async_copy(source.at[slot, :, rows], out.at[:, pl.ds(0, BLK)], sems.at[0])

    def from_high(source):
        rows = pl.ds(0, BLK)
        return pltpu.make_async_copy(source.at[slot, :, rows], out.at[:, pl.ds(BLK, BLK)], sems.at[1])

    @pl.when(x_at == 0)
    def _():
        from_low(lows[1]).start()

    @pl.when(x_at != 0)
    def _():
        from_low(lows[0]).start()

    @pl.when(x_at == XN - 1)
    def _():
        from_high(highs[1]).start()

    @pl.when(x_at != XN - 1)
    def _():
        from_high(highs[0]).start()

    from_low(lows[0]).wait()
    from_high(highs[0]).wait()


def corner(own_pair, place, lows, highs):
    shape = lows[0].shape
    return pl.pallas_call(
        functools.partial(corner_kernel, own_pair),
        in_specs=[SMEM] + [ANY] * (len(lows) + len(highs)),
        out_specs=VMEM,
        out_shape=jax.ShapeDtypeStruct((2, 2 * BLK, shape[3]), jnp.bfloat16),
        scratch_shapes=[pltpu.SemaphoreType.DMA((2,))],
        compiler_params=pltpu.CompilerParams(vmem_limit_bytes=4 * 2**20),
    )(place, *lows, *highs)


def head_scores(query, keys, bias):
    scores = jnp.concatenate(
        [
            lax.dot_general(query, k, (((1,), (1,)), ((), ())), preferred_element_type=jnp.float32)
            for k in keys
        ],
        axis=1,
    )
    return jnp.concatenate([scores[:BLK] + bias[0:1], scores[BLK:] + bias[1:2]], axis=0)


def own_bias(bias_ref, frame, near):
    start = (near[0] - frame + REACH) * 2 * BLK
    return bias_ref[frame, :, start : start + len(near) * 2 * BLK]


def weighted(weights, values):
    rounded = weights.astype(jnp.bfloat16)
    start, out = 0, 0
    for v in values:
        out = out + jnp.dot(
            rounded[:, start : start + v.shape[0]], v, preferred_element_type=jnp.float32
        )
        start += v.shape[0]
    return out


def gather_queries(me, queries, got):
    for slot, array in enumerate(got):
        queries[me ^ slot] = array[2]


def own_kernel(
    at_ref, bias_ref, got0, got1, got2, got3, own, oth, after0, after1, out_ref, top_ref, sum_ref, keys, values, queries,
):
    del after0, after1
    me = at_ref[0]
    gather_queries(me, queries, (got0, got1, got2, got3))
    for which, store in ((0, keys), (1, values)):
        for slot in range(2):
            store[me ^ slot] = own[slot, which]
            store[me ^ slot ^ 2] = oth[slot, which]
    near = [range(max(frame - REACH, 0), min(frame + REACH + 1, GROUP)) for frame in range(GROUP)]
    for head in range(own.shape[3] // HDIM):
        lanes = slice(head * HDIM, (head + 1) * HDIM)
        scores = [
            head_scores(
                queries[frame, :, lanes],
                [keys[at, :, lanes] for at in near[frame]],
                own_bias(bias_ref, frame, near[frame]),
            )
            for frame in range(GROUP)
        ]
        tops = [jnp.max(s, axis=1, keepdims=True) for s in scores]
        weights = [jnp.exp2((s - top) * SCALE) for s, top in zip(scores, tops)]
        totals = [jnp.sum(w, axis=1, keepdims=True) for w in weights]
        for frame in range(GROUP):
            out_ref[frame, :, lanes] = weighted(
                weights[frame], [values[at, :, lanes] for at in near[frame]]
            )
            shape = (tops[frame].shape[0], HDIM)
            top_ref[frame, :, lanes] = jnp.broadcast_to(tops[frame], shape)
            sum_ref[frame, :, lanes] = jnp.broadcast_to(totals[frame], shape)


def halo_kernel(
    frames, at_ref, bias_ref, got0, got1, got2, got3, sofar, top_in, sum_in,
    low_own, high_own, second, low_oth, high_oth, direct, z_own, z_oth, *rest
):
    corners, (out_ref, keys, values, queries, z_keys, z_values) = rest[:-6], rest[-6:]
    me, x_at = at_ref[0], at_ref[1]
    upper = me >= 2
    length = low_own.shape[2]
    below, above = slice(0, length), slice(length, 2 * length)
    gather_queries(me, queries, (got0, got1, got2, got3))
    for which, store in ((0, keys), (1, values)):
        for slot in range(2):
            at = 1 + (me ^ slot)
            store[at, below] = jnp.where(x_at == 0, second[slot, which], low_own[slot, which])
            store[at, above] = jnp.where(
                x_at == XN - 1, second[slot, which], high_own[slot, which]
            )
            at = 1 + (me ^ slot ^ 2)
            store[at, below] = jnp.where(x_at == 0, direct[slot, which], low_oth[slot, which])
            store[at, above] = jnp.where(x_at == XN - 1, direct[slot, which], high_oth[slot, which])
        z_store = z_keys if which == 0 else z_values
        for slot in range(2):
            at = me ^ slot
            z_store[jnp.where(upper, at - 2, at + 2)] = z_own[slot, which]
            at = at ^ 2
            z_store[jnp.where(upper, at + 2, at - 2)] = z_oth[slot, which]
        for arrived, at in zip(corners, (jnp.where(upper, 0, 5), jnp.where(upper, 5, 0))):
            store[at, length - BLK : length + BLK] = arrived[which]
    reaches = [(step, (REACH - abs(step)) * BLK) for step in HALO_STEPS]
    units = [
        (at, frame, slice(head * HDIM, (head + 1) * HDIM))
        for head in range(low_own.shape[3] // HDIM)
        for at, frame in enumerate(frames)
    ]

    z_frames = (-2, -1, GROUP, GROUP + 1)
    z_near = [[z for z in z_frames if abs(z - frame) <= REACH] for frame in range(GROUP)]

    def spans(store, z_store, frame, lanes):
        return [z_store[z_frames.index(z), :, lanes] for z in z_near[frame]] + [
            store[frame + 1 + step, length - reach : length + reach, lanes]
            for step, reach in reaches
        ]

    biases = {
        frame: jnp.concatenate(
            [own_bias(bias_ref, frame, z_near[frame]), bias_ref[frame, :, OWN_KEYS:]], axis=1
        )
        for frame in frames
    }
    scores = [
        head_scores(queries[frame, :, lanes], spans(keys, z_keys, frame, lanes), biases[frame])
        for _, frame, lanes in units
    ]
    tops = [
        jnp.maximum(top_in[frame, :, lanes], jnp.max(s, axis=1, keepdims=True))
        for s, (_, frame, lanes) in zip(scores, units)
    ]
    weights = [jnp.exp2((s - top[:, 0:1]) * SCALE) for s, top in zip(scores, tops)]
    totals = [jnp.sum(w, axis=1, keepdims=True) for w in weights]
    for top, w, total, (at, frame, lanes) in zip(tops, weights, totals, units):
        again = jnp.exp2((top_in[frame, :, lanes] - top) * SCALE)
        out = sofar[frame, :, lanes] * again + weighted(
            w, spans(values, z_values, frame, lanes)
        )
        total = sum_in[frame, :, lanes] * again + total
        out_ref[at, :, lanes] = (out / total).astype(jnp.bfloat16)


def attend(kernel, out_shape, scratches, work, place, bias, arrays, after=()):
    length, width = arrays[0].shape[1:]
    return pl.pallas_call(
        kernel,
        in_specs=[SMEM] + [VMEM] * (1 + len(arrays)) + [ANY] * len(after),
        out_specs=jax.tree.map(lambda _: VMEM, out_shape),
        out_shape=out_shape,
        scratch_shapes=[pltpu.VMEM(scratch, jnp.bfloat16) for scratch in scratches],
        compiler_params=pltpu.CompilerParams(vmem_limit_bytes=24 * 2**20),
        cost_estimate=pl.CostEstimate(
            flops=4 * work * width * length, bytes_accessed=8_000_000,
            transcendentals=work * width * length // HDIM,
        ),
    )(place, bias, *arrays, *after)


def shards(frame_total, row_total, queries, key_states, value_states, radial_mask):
    length, width = queries.shape[1:]
    part = width // GROUP
    frame_at = lax.axis_index("frame")
    row_at = lax.axis_index("row")
    me = frame_at % GROUP
    x_at = row_at % XN
    place = jnp.stack([me, x_at]).astype(jnp.int32)

    def send(array, target):
        return lax.ppermute(array, AXES, pairs_of(frame_total, row_total, target))

    packed = pl.pallas_call(
        pack_kernel,
        in_specs=[SMEM] + [ANY] * 3,
        out_specs=[VMEM] * GROUP,
        out_shape=[jax.ShapeDtypeStruct((3, length, part), jnp.bfloat16)] * GROUP,
        scratch_shapes=[pltpu.SemaphoreType.DMA((GROUP, 3))],
        compiler_params=pltpu.CompilerParams(vmem_limit_bytes=56 * 2**20),
    )(place, queries[0], key_states[0], value_states[0])

    def flip(bits):
        return lambda f, r: (f ^ bits, r)

    groups = [list(range(f, f + GROUP)) for f in range(0, frame_total, GROUP)]
    arrived = [packed[0]] + [send(packed[s], flip(s)) for s in range(1, GROUP)]
    own = jnp.stack([arrived[0][:2], arrived[1][:2]])

    def row_first(by):
        edge = XN - 1 if by > 0 else 0
        return lambda f, r: (f, r + by) if r % XN != edge else (f, r - by * (XN - 1))

    def row_second(f, r):
        return (f, r + XN) if r % XN == 0 else (f, r - XN) if r % XN == XN - 1 else None

    def row_inner(by):
        edge = XN - 1 if by > 0 else 0
        return lambda f, r: (f, r + by) if r % XN != edge else None

    def row_across(f, r):
        return (f, r + 1) if r % XN == XN - 1 else (f, r - 1) if r % XN == 0 else None

    def z_target(own_pair):
        def target(f, r):
            up = (f % GROUP >= 2) == own_pair
            return (f + GROUP if up else f - GROUP, r)

        return target

    low_own, high_own = send(own, row_first(1)), send(own, row_first(-1))
    z_own = send(own, z_target(True))
    oth = join(arrived[2], arrived[3])
    direct = send(oth, row_across)
    wrapped = wrapped_of(place, low_own, high_own, oth)
    second = send(wrapped, row_second)

    bias = bias_of(radial_mask, frame_at - me, row_at, frame_total)
    sums = [jax.ShapeDtypeStruct((GROUP, length, part), jnp.float32)] * 3
    partial = attend(
        own_kernel, sums, [(GROUP, length, part)] * 3, 14 * length, place, bias,
        arrived + [own, oth], [wrapped, z_own],
    )
    later = join(arrived[2], arrived[3], partial[0])
    low_oth, high_oth = send(later, row_inner(1)), send(later, row_inner(-1))
    z_oth = send(later, z_target(False))
    c_own = corner(True, place, [low_own, second], [high_own, second])
    c_oth = corner(False, place, [low_oth, direct], [high_oth, direct])
    c_own, c_oth = send(c_own, z_target(True)), send(c_oth, z_target(False))

    arrays = arrived + list(partial) + [low_own, high_own, second, low_oth, high_oth, direct]
    arrays += [z_own, z_oth]
    group_shape = (GROUP, length, part)
    half = jax.ShapeDtypeStruct((2, length, part), jnp.bfloat16)
    halo_keys = bias.shape[2] - OWN_KEYS
    middle, edge = [
        attend(
            functools.partial(halo_kernel, frames), half,
            [(GROUP + 2, 2 * length, part)] * 2 + [group_shape] * 3, 2 * halo_keys, place, bias, arrays + corners,
        )
        for frames, corners in (((1, 2), []), ((0, 3), [c_own, c_oth]))
    ]
    by_frame = jnp.stack([edge[0], middle[0], middle[1], edge[1]])
    back = lax.all_to_all(by_frame, "frame", 0, 0, axis_index_groups=groups)
    result = pl.pallas_call(
        unpack_kernel,
        in_specs=[ANY],
        out_specs=ANY,
        out_shape=jax.ShapeDtypeStruct((length, width), jnp.bfloat16),
        scratch_shapes=[pltpu.SemaphoreType.DMA((GROUP,))],
        compiler_params=pltpu.CompilerParams(vmem_limit_bytes=4 * 2**20),
    )(back)
    return result[None]


def solution(mesh):
    sharded = P("frame", "row", None)
    body = functools.partial(shards, mesh.shape["frame"], mesh.shape["row"])
    return jax.shard_map(
        body, mesh=mesh, in_specs=(sharded, sharded, sharded, P()), out_specs=sharded, check_vma=False
    )
```

time: 120 us -> 109 us (0.908)
  Pallas kernels: 30.2 us -> 18.5 us
  blocking collectives: 12.7 us -> 17.1 us
  starting transfers between devices: 40.7 us -> 38.8 us
  local copies, waits for them, and re-layouts: 4.73 us -> 3.23 us
    pallas_call x3 -> x6, Pallas kernels: 23.3 us -> 12.3 us  [the longest x3 11.1 us: attend(): pl.pallas_call(kernel, in_specs=[SMEM] + [VMEM] * (1 + len(arrays)) + [AN...]
    all_to_all x1, blocking collectives: 12.7 us -> 17.1 us  [shards(): back = lax.all_to_all(by_frame, 'frame', 0, 0, axis_index_groups=groups)]
    unnamed x21 -> x13, local copies, waits for them, and re-layouts: 3.17 us -> 0.16 us
    ppermute x13, starting transfers between devices: 40.7 us -> 38.8 us  [send(): return lax.ppermute(array, AXES, pairs_of(frame_total, row_total, target))]
  transfers between devices with their start and end apart: 13 -> 13, of which waited for: 4 -> 4; matrix products, arithmetic and copies ran while one was open for 2% -> 4% of each run, Pallas kernels for 15% -> 9%
where the time goes in v2:
time: 109 us
  starting transfers between devices  38.8 us (36%)
  waiting for transfers between devices  28.9 us (27%)
  Pallas kernels  18.5 us (17%)
  blocking collectives  17.1 us (16%)
  local copies, waits for them, and re-layouts  3.23 us (3%)
  other arithmetic  1.86 us (2%)
    ppermute x13, starting transfers between devices, send(): return lax.ppermute(array, AXES, pairs_of(frame_total, row_total, target))  38.8 us
    ppermute x13, waiting for transfers between devices, send(): return lax.ppermute(array, AXES, pairs_of(frame_total, row_total, target))  28.9 us
    all_to_all x1, blocking collectives, shards(): back = lax.all_to_all(by_frame, 'frame', 0, 0, axis_index_groups=groups)  17.1 us
    pallas_call x3, Pallas kernels, attend(): pl.pallas_call(kernel, in_specs=[SMEM] + [VMEM] * (1 + len(arrays)) + [AN...  11.1 us
    pallas_call x1, Pallas kernels, shards(): pl.pallas_call(pack_kernel, in_specs=[SMEM] + [ANY] * 3, out_specs=[VMEM]...  3.66 us
  transfers between devices with their start and end apart: 13, of which 4 were waited for; matrix products, arithmetic and copies ran while one was open for 4% of the time, Pallas kernels for 9%

profile of v2, /device:TPU:240, one launch (start us, length us, event | category | flops | bytes accessed | tf_op | source)
XLA Modules:
  0.0 108.6 jit_solution(6830882134392198414)
XLA Ops:
  0.0 0.7 pad_add_fusion.at_ref
  0.7 3.7 %shard_map.73 = (bf16[3,128,640]{2,1,0:T(8,128)(2,1)}, bf16[3,128,640]{2,1,0:T(8,128)(2,1)}, bf16[3,128,640]{2,1,0:T(8,128)(2,1)}, bf16[3,128,640]{2,1,0:T(8,128)(2,1)}) custom-call(s32[2]{0:T(128)} %pad_add_fusion.at_ref, bf16[128,2560]{1,0:T(8,128)(2,1)} %bitcast.10, bf16[128,2560]{1,0:T(8,128)(2,1)} %bitcast.11, bf16[128,2560]{1,0:T(8,128)(2,1)} %bitcast.12), custom_call_target="tpu_custom_call" | custom-call | tf_op jit(solution)/shard_map/pallas_call | solution.py:362
  4.3 1.9 %collective-permute-start = (bf16[3,128,640]{2,1,0:T(8,128)(2,1)}, bf16[3,128,640]{2,1,0:T(8,128)(2,1)S(1)}, u32[]{:S(2)}, u32[]{:S(2)}) collective-permute-start(bf16[3,128,640]{2,1,0:T(8,128)(2,1)} %get-tuple-element.13), channel_id=1, source_target_pairs={{0,16},{1,17},{2,18},{3,19},{4,20},{5,21},{6,22},{7,23},{8,24},{9,... | collective-permute-start | bytes 1474568 | tf_op jit(solution)/shard_map/ppermute | solution.py:360
  6.3 2.6 %collective-permute-start.1 = (bf16[3,128,640]{2,1,0:T(8,128)(2,1)}, bf16[3,128,640]{2,1,0:T(8,128)(2,1)S(1)}, u32[]{:S(2)}, u32[]{:S(2)}) collective-permute-start(bf16[3,128,640]{2,1,0:T(8,128)(2,1)} %get-tuple-element.14), channel_id=1, source_target_pairs={{0,32},{1,33},{2,34},{3,35},{4,36},{5,37},{6,38},{7,39},{8,40},{9,... | collective-permute-start | bytes 1474568 | tf_op jit(solution)/shard_map/ppermute | solution.py:360
  8.8 3.1 %collective-permute-start.2 = (bf16[3,128,640]{2,1,0:T(8,128)(2,1)}, bf16[3,128,640]{2,1,0:T(8,128)(2,1)S(1)}, u32[]{:S(2)}, u32[]{:S(2)}) collective-permute-start(bf16[3,128,640]{2,1,0:T(8,128)(2,1)} %get-tuple-element.15), channel_id=1, source_target_pairs={{0,48},{1,49},{2,50},{3,51},{4,52},{5,53},{6,54},{7,55},{8,56},{9,... | collective-permute-start | bytes 1474568 | tf_op jit(solution)/shard_map/ppermute | solution.py:360
  12.5 1.0 slice_bitcast_fusion.1
  13.6 0.9 pad_maximum_fusion.own
  14.5 3.4 %collective-permute-start.3 = (bf16[2,2,128,640]{3,2,1,0:T(8,128)(2,1)}, bf16[2,2,128,640]{3,2,1,0:T(8,128)(2,1)S(1)}, u32[]{:S(2)}, u32[]{:S(2)}) collective-permute-start(bf16[2,2,128,640]{3,2,1,0:T(8,128)(2,1)} %pad_maximum_fusion.own), channel_id=1, source_target_pairs={{0,1},{1,2},{2,3},{3,0},{4,5},{5,6},{6,7},{7,4},{8,9},{9,10},{10,1... | collective-permute-start | bytes 1966088 | tf_op jit(solution)/shard_map/ppermute | solution.py:360
  17.9 3.7 %collective-permute-start.4 = (bf16[2,2,128,640]{3,2,1,0:T(8,128)(2,1)}, bf16[2,2,128,640]{3,2,1,0:T(8,128)(2,1)S(1)}, u32[]{:S(2)}, u32[]{:S(2)}) collective-permute-start(bf16[2,2,128,640]{3,2,1,0:T(8,128)(2,1)} %pad_maximum_fusion.own), channel_id=1, source_target_pairs={{0,3},{1,0},{2,1},{3,2},{4,7},{5,4},{6,5},{7,6},{8,11},{9,8},{10,9... | collective-permute-start | bytes 1966088 | tf_op jit(solution)/shard_map/ppermute | solution.py:360
  21.5 1.9 %collective-permute-start.5 = (bf16[2,2,128,640]{3,2,1,0:T(8,128)(2,1)}, bf16[2,2,128,640]{3,2,1,0:T(8,128)(2,1)S(1)}, u32[]{:S(2)}, u32[]{:S(2)}) collective-permute-start(bf16[2,2,128,640]{3,2,1,0:T(8,128)(2,1)} %pad_maximum_fusion.own), channel_id=1, source_target_pairs={{32,96},{33,97},{34,98},{35,99},{36,100},{37,101},{38,102},{39,103... | collective-permute-start | bytes 1966088 | tf_op jit(solution)/shard_map/ppermute | solution.py:360
  23.6 0.7 broadcast_in_dim.21
  24.3 1.0 reshape.59.bias_ref
  25.3 6.8 %collective-permute-done.2.second.got3 = bf16[3,128,640]{2,1,0:T(8,128)(2,1)S(1)} collective-permute-done((bf16[3,128,640]{2,1,0:T(8,128)(2,1)}, bf16[3,128,640]{2,1,0:T(8,128)(2,1)S(1)}, u32[]{:S(2)}, u32[]{:S(2)}) %collective-permute-start.2) | collective-permute-done | bytes 491552 | tf_op jit(solution)/shard_map/ppermute | solution.py:360
  32.4 6.4 %collective-permute-start.9 = (bf16[2,2,128,640]{3,2,1,0:T(8,128)(2,1)S(1)}, bf16[2,2,128,640]{3,2,1,0:T(8,128)(2,1)S(1)}, u32[]{:S(2)}, u32[]{:S(2)}) collective-permute-start(bf16[2,2,128,640]{3,2,1,0:T(8,128)(2,1)S(1)} %shard_map.74.after.oth), channel_id=1, source_target_pairs={{3,4},{4,3},{7,8},{8,7},{11,12},{12,11},{19,20},{20,19},{23,24},{2... | collective-permute-start | bytes 1966088 | tf_op jit(solution)/shard_map/ppermute | solution.py:360
  38.8 0.8 shard_map.75.after0
  39.5 1.3 %collective-permute-start.6 = (bf16[2,2,128,640]{3,2,1,0:T(8,128)(2,1)S(1)}, bf16[2,2,128,640]{3,2,1,0:T(8,128)(2,1)S(1)}, u32[]{:S(2)}, u32[]{:S(2)}) collective-permute-start(bf16[2,2,128,640]{3,2,1,0:T(8,128)(2,1)S(1)} %shard_map.75.after0), channel_id=1, source_target_pairs={{0,4},{4,8},{7,3},{8,12},{11,7},{15,11},{16,20},{20,24},{23,19},{2... | collective-permute-start | bytes 1966088 | tf_op jit(solution)/shard_map/ppermute | solution.py:360
  40.8 1.0 collective-permute-done.5.after1.z_own
  41.9 4.0 %shard_map.76 = (f32[4,128,640]{2,1,0:T(8,128)S(1)}, f32[4,128,640]{2,1,0:T(8,128)S(1)}, f32[4,128,640]{2,1,0:T(8,128)S(1)}) custom-call(s32[2]{0:T(128)S(1)} %copy-done.2, f32[4,2,1152]{2,1,0:T(2,128)S(1)} %reshape.59.bias_ref, bf16[3,128,640]{2,1,0:T(8,128)(2,1)S(1)} %copy-done.1, bf16[3,128,640]{2,1,0:T(8,128)(2,1)S(1)} %collective-permute-done.got1, ...), custom_call_target="tpu_custom_call" | custom-call | flops 587202560 | bytes 8000000 | tf_op jit(solution)/shard_map/pallas_call | solution.py:336
  45.9 0.2 shard_map.77
  46.1 2.2 %collective-permute-start.7 = (bf16[2,2,128,640]{3,2,1,0:T(8,128)(2,1)S(1)}, bf16[2,2,128,640]{3,2,1,0:T(8,128)(2,1)S(1)}, u32[]{:S(2)}, u32[]{:S(2)}) collective-permute-start(bf16[2,2,128,640]{3,2,1,0:T(8,128)(2,1)S(1)} %shard_map.77), channel_id=1, source_target_pairs={{0,1},{1,2},{2,3},{4,5},{5,6},{6,7},{8,9},{9,10},{10,11},{12,13},{... | collective-permute-start | bytes 1966088 | tf_op jit(solution)/shard_map/ppermute | solution.py:360
  48.4 1.3 %collective-permute-start.8 = (bf16[2,2,128,640]{3,2,1,0:T(8,128)(2,1)S(1)}, bf16[2,2,128,640]{3,2,1,0:T(8,128)(2,1)S(1)}, u32[]{:S(2)}, u32[]{:S(2)}) collective-permute-start(bf16[2,2,128,640]{3,2,1,0:T(8,128)(2,1)S(1)} %shard_map.77), channel_id=1, source_target_pairs={{1,0},{2,1},{3,2},{5,4},{6,5},{7,6},{9,8},{10,9},{11,10},{13,12},{... | collective-permute-start | bytes 1966088 | tf_op jit(solution)/shard_map/ppermute | solution.py:360
  49.7 3.6 %collective-permute-start.10 = (bf16[2,2,128,640]{3,2,1,0:T(8,128)(2,1)S(1)}, bf16[2,2,128,640]{3,2,1,0:T(8,128)(2,1)S(1)}, u32[]{:S(2)}, u32[]{:S(2)}) collective-permute-start(bf16[2,2,128,640]{3,2,1,0:T(8,128)(2,1)S(1)} %shard_map.77), channel_id=1, source_target_pairs={{0,64},{1,65},{2,66},{3,67},{4,68},{5,69},{6,70},{7,71},{8,72},{9,... | collective-permute-start | bytes 1966088 | tf_op jit(solution)/shard_map/ppermute | solution.py:360
  53.3 20.0 %collective-permute-done.6.refs_1_.refs_3_.second = bf16[2,2,128,640]{3,2,1,0:T(8,128)(2,1)S(1)} collective-permute-done((bf16[2,2,128,640]{3,2,1,0:T(8,128)(2,1)S(1)}, bf16[2,2,128,640]{3,2,1,0:T(8,128)(2,1)S(1)}, u32[]{:S(2)}, u32[]{:S(2)}) %collective-permute-start.6) | collective-permute-done | bytes 655392 | tf_op jit(solution)/shard_map/ppermute | solution.py:360
  73.3 0.8 shard_map.78
  74.1 1.9 %collective-permute-start.11 = (bf16[2,128,640]{2,1,0:T(8,128)(2,1)S(1)}, bf16[2,128,640]{2,1,0:T(8,128)(2,1)S(1)}, u32[]{:S(2)}, u32[]{:S(2)}) collective-permute-start(bf16[2,128,640]{2,1,0:T(8,128)(2,1)S(1)} %shard_map.78), channel_id=1, source_target_pairs={{32,96},{33,97},{34,98},{35,99},{36,100},{37,101},{38,102},{39,103... | collective-permute-start | bytes 983048 | tf_op jit(solution)/shard_map/ppermute | solution.py:360
  76.1 0.8 shard_map.79
  76.9 5.5 %collective-permute-start.12 = (bf16[2,128,640]{2,1,0:T(8,128)(2,1)S(1)}, bf16[2,128,640]{2,1,0:T(8,128)(2,1)S(1)}, u32[]{:S(2)}, u32[]{:S(2)}) collective-permute-start(bf16[2,128,640]{2,1,0:T(8,128)(2,1)S(1)} %shard_map.79), channel_id=1, source_target_pairs={{0,64},{1,65},{2,66},{3,67},{4,68},{5,69},{6,70},{7,71},{8,72},{9,... | collective-permute-start | bytes 983048 | tf_op jit(solution)/shard_map/ppermute | solution.py:360
  82.4 3.5 %shard_map.81 = bf16[2,128,640]{2,1,0:T(8,128)(2,1)S(1)} custom-call(s32[2]{0:T(128)S(1)} %copy-done.2, f32[4,2,1152]{2,1,0:T(2,128)S(1)} %reshape.59.bias_ref, bf16[3,128,640]{2,1,0:T(8,128)(2,1)S(1)} %copy-done.1, bf16[3,128,640]{2,1,0:T(8,128)(2,1)S(1)} %collective-permute-done.got1, bf16[3,128,640]{2,1,0:T(8,128)(2,1)S(1)} %collective-permute-done.1.first.got2, ...), custom_call_target="tpu_custom_call" | custom-call | flops 335544320 | bytes 8000000 | tf_op jit(solution)/shard_map/pallas_call | solution.py:336
  85.9 1.1 collective-permute-done.12.rest_1_
  86.9 3.6 %shard_map.80 = bf16[2,128,640]{2,1,0:T(8,128)(2,1)S(1)} custom-call(s32[2]{0:T(128)S(1)} %copy-done.2, f32[4,2,1152]{2,1,0:T(2,128)S(1)} %reshape.59.bias_ref, bf16[3,128,640]{2,1,0:T(8,128)(2,1)S(1)} %copy-done.1, bf16[3,128,640]{2,1,0:T(8,128)(2,1)S(1)} %collective-permute-done.got1, bf16[3,128,640]{2,1,0:T(8,128)(2,1)S(1)} %collective-permute-done.1.first.got2, ...), custom_call_target="tpu_custom_call" | custom-call | flops 335544320 | bytes 8000000 | tf_op jit(solution)/shard_map/pallas_call | solution.py:336
  90.7 17.1 %all_to_all.5.in_ref = bf16[4,128,640]{2,1,0:T(8,128)(2,1)S(1)} all-to-all(bf16[4,128,640]{2,1,0:T(8,128)(2,1)S(1)} %pad_maximum_fusion.1), channel_id=1, replica_groups={{0,16,32,48},{64,80,96,112},{128,144,160,176},{192,208,224,240},{256,27..., dimensions={0} | all-to-all | bytes 1310720 | tf_op jit(solution)/shard_map/all_to_all | solution.py:432
  107.8 0.9 shard_map.82
  (37 shorter events, 1.0 us)
Async XLA Ops:
  0.0 11.9 %copy-start = (s32[5,32,5]{1,2,0:T(8,128)S(1)}, s32[5,32,5]{1,2,0:T(8,128)}, u32[]{:S(2)}) copy-start(s32[5,32,5]{1,2,0:T(8,128)} %param.10) | copy-start | bytes 9604
  0.0 12.3 %copy-start.3 = (f32[2,18,50]{2,0,1:T(2,128)S(1)}, f32[2,18,50]{2,0,1:T(2,128)}, u32[]{:S(2)}) copy-start(f32[2,18,50]{2,0,1:T(2,128)} %constant.46.clone) | copy-start | bytes 21604
  4.3 9.2 %collective-permute-start = (bf16[3,128,640]{2,1,0:T(8,128)(2,1)}, bf16[3,128,640]{2,1,0:T(8,128)(2,1)S(1)}, u32[]{:S(2)}, u32[]{:S(2)}) collective-permute-start(bf16[3,128,640]{2,1,0:T(8,128)(2,1)} %get-tuple-element.13), channel_id=1, source_target_pairs={{0,16},{1,17},{2,18},{3,19},{4,20},{5,21},{6,22},{7,23},{8,24},{9,... | collective-permute-start | bytes 1474568 | tf_op jit(solution)/shard_map/ppermute | solution.py:360
  6.3 19.1 %collective-permute-start.1 = (bf16[3,128,640]{2,1,0:T(8,128)(2,1)}, bf16[3,128,640]{2,1,0:T(8,128)(2,1)S(1)}, u32[]{:S(2)}, u32[]{:S(2)}) collective-permute-start(bf16[3,128,640]{2,1,0:T(8,128)(2,1)} %get-tuple-element.14), channel_id=1, source_target_pairs={{0,32},{1,33},{2,34},{3,35},{4,36},{5,37},{6,38},{7,39},{8,40},{9,... | collective-permute-start | bytes 1474568 | tf_op jit(solution)/shard_map/ppermute | solution.py:360
  8.8 23.3 %collective-permute-start.2 = (bf16[3,128,640]{2,1,0:T(8,128)(2,1)}, bf16[3,128,640]{2,1,0:T(8,128)(2,1)S(1)}, u32[]{:S(2)}, u32[]{:S(2)}) collective-permute-start(bf16[3,128,640]{2,1,0:T(8,128)(2,1)} %get-tuple-element.15), channel_id=1, source_target_pairs={{0,48},{1,49},{2,50},{3,51},{4,52},{5,53},{6,54},{7,55},{8,56},{9,... | collective-permute-start | bytes 1474568 | tf_op jit(solution)/shard_map/ppermute | solution.py:360
  12.5 11.0 %copy-start.5 = (s32[18]{0:T(128)S(1)}, s32[18]{0:T(128)}, u32[]{:S(2)}) copy-start(s32[18]{0:T(128)} %constant.48.clone) | copy-start | bytes 220
  12.5 11.0 %copy-start.4 = (s32[18]{0:T(128)S(1)}, s32[18]{0:T(128)}, u32[]{:S(2)}) copy-start(s32[18]{0:T(128)} %constant.47.clone) | copy-start | bytes 220
  13.6 25.2 %copy-start.2 = (s32[2]{0:T(128)S(1)}, s32[2]{0:T(128)}, u32[]{:S(2)}) copy-start(s32[2]{0:T(128)} %pad_add_fusion.at_ref) | copy-start | bytes 28
  14.5 24.3 %collective-permute-start.3 = (bf16[2,2,128,640]{3,2,1,0:T(8,128)(2,1)}, bf16[2,2,128,640]{3,2,1,0:T(8,128)(2,1)S(1)}, u32[]{:S(2)}, u32[]{:S(2)}) collective-permute-start(bf16[2,2,128,640]{3,2,1,0:T(8,128)(2,1)} %pad_maximum_fusion.own), channel_id=1, source_target_pairs={{0,1},{1,2},{2,3},{3,0},{4,5},{5,6},{6,7},{7,4},{8,9},{9,10},{10,1... | collective-permute-start | bytes 1966088 | tf_op jit(solution)/shard_map/ppermute | solution.py:360
  17.9 20.9 %collective-permute-start.4 = (bf16[2,2,128,640]{3,2,1,0:T(8,128)(2,1)}, bf16[2,2,128,640]{3,2,1,0:T(8,128)(2,1)S(1)}, u32[]{:S(2)}, u32[]{:S(2)}) collective-permute-start(bf16[2,2,128,640]{3,2,1,0:T(8,128)(2,1)} %pad_maximum_fusion.own), channel_id=1, source_target_pairs={{0,3},{1,0},{2,1},{3,2},{4,7},{5,4},{6,5},{7,6},{8,11},{9,8},{10,9... | collective-permute-start | bytes 1966088 | tf_op jit(solution)/shard_map/ppermute | solution.py:360
  21.5 20.3 %collective-permute-start.5 = (bf16[2,2,128,640]{3,2,1,0:T(8,128)(2,1)}, bf16[2,2,128,640]{3,2,1,0:T(8,128)(2,1)S(1)}, u32[]{:S(2)}, u32[]{:S(2)}) collective-permute-start(bf16[2,2,128,640]{3,2,1,0:T(8,128)(2,1)} %pad_maximum_fusion.own), channel_id=1, source_target_pairs={{32,96},{33,97},{34,98},{35,99},{36,100},{37,101},{38,102},{39,103... | collective-permute-start | bytes 1966088 | tf_op jit(solution)/shard_map/ppermute | solution.py:360
  32.3 9.5 %copy-start.1 = (bf16[3,128,640]{2,1,0:T(8,128)(2,1)S(1)}, bf16[3,128,640]{2,1,0:T(8,128)(2,1)}, u32[]{:S(2)}) copy-start(bf16[3,128,640]{2,1,0:T(8,128)(2,1)} %get-tuple-element.12.got0) | copy-start | bytes 1474564
  32.4 43.7 %collective-permute-start.9 = (bf16[2,2,128,640]{3,2,1,0:T(8,128)(2,1)S(1)}, bf16[2,2,128,640]{3,2,1,0:T(8,128)(2,1)S(1)}, u32[]{:S(2)}, u32[]{:S(2)}) collective-permute-start(bf16[2,2,128,640]{3,2,1,0:T(8,128)(2,1)S(1)} %shard_map.74.after.oth), channel_id=1, source_target_pairs={{3,4},{4,3},{7,8},{8,7},{11,12},{12,11},{19,20},{20,19},{23,24},{2... | collective-permute-start | bytes 1966088 | tf_op jit(solution)/shard_map/ppermute | solution.py:360
  39.5 33.8 %collective-permute-start.6 = (bf16[2,2,128,640]{3,2,1,0:T(8,128)(2,1)S(1)}, bf16[2,2,128,640]{3,2,1,0:T(8,128)(2,1)S(1)}, u32[]{:S(2)}, u32[]{:S(2)}) collective-permute-start(bf16[2,2,128,640]{3,2,1,0:T(8,128)(2,1)S(1)} %shard_map.75.after0), channel_id=1, source_target_pairs={{0,4},{4,8},{7,3},{8,12},{11,7},{15,11},{16,20},{20,24},{23,19},{2... | collective-permute-start | bytes 1966088 | tf_op jit(solution)/shard_map/ppermute | solution.py:360
  46.1 29.9 %collective-permute-start.7 = (bf16[2,2,128,640]{3,2,1,0:T(8,128)(2,1)S(1)}, bf16[2,2,128,640]{3,2,1,0:T(8,128)(2,1)S(1)}, u32[]{:S(2)}, u32[]{:S(2)}) collective-permute-start(bf16[2,2,128,640]{3,2,1,0:T(8,128)(2,1)S(1)} %shard_map.77), channel_id=1, source_target_pairs={{0,1},{1,2},{2,3},{4,5},{5,6},{6,7},{8,9},{9,10},{10,11},{12,13},{... | collective-permute-start | bytes 1966088 | tf_op jit(solution)/shard_map/ppermute | solution.py:360
  48.4 27.7 %collective-permute-start.8 = (bf16[2,2,128,640]{3,2,1,0:T(8,128)(2,1)S(1)}, bf16[2,2,128,640]{3,2,1,0:T(8,128)(2,1)S(1)}, u32[]{:S(2)}, u32[]{:S(2)}) collective-permute-start(bf16[2,2,128,640]{3,2,1,0:T(8,128)(2,1)S(1)} %shard_map.77), channel_id=1, source_target_pairs={{1,0},{2,1},{3,2},{5,4},{6,5},{7,6},{9,8},{10,9},{11,10},{13,12},{... | collective-permute-start | bytes 1966088 | tf_op jit(solution)/shard_map/ppermute | solution.py:360
  49.7 32.7 %collective-permute-start.10 = (bf16[2,2,128,640]{3,2,1,0:T(8,128)(2,1)S(1)}, bf16[2,2,128,640]{3,2,1,0:T(8,128)(2,1)S(1)}, u32[]{:S(2)}, u32[]{:S(2)}) collective-permute-start(bf16[2,2,128,640]{3,2,1,0:T(8,128)(2,1)S(1)} %shard_map.77), channel_id=1, source_target_pairs={{0,64},{1,65},{2,66},{3,67},{4,68},{5,69},{6,70},{7,71},{8,72},{9,... | collective-permute-start | bytes 1966088 | tf_op jit(solution)/shard_map/ppermute | solution.py:360
  74.1 11.7 %collective-permute-start.11 = (bf16[2,128,640]{2,1,0:T(8,128)(2,1)S(1)}, bf16[2,128,640]{2,1,0:T(8,128)(2,1)S(1)}, u32[]{:S(2)}, u32[]{:S(2)}) collective-permute-start(bf16[2,128,640]{2,1,0:T(8,128)(2,1)S(1)} %shard_map.78), channel_id=1, source_target_pairs={{32,96},{33,97},{34,98},{35,99},{36,100},{37,101},{38,102},{39,103... | collective-permute-start | bytes 983048 | tf_op jit(solution)/shard_map/ppermute | solution.py:360
  76.9 10.1 %collective-permute-start.12 = (bf16[2,128,640]{2,1,0:T(8,128)(2,1)S(1)}, bf16[2,128,640]{2,1,0:T(8,128)(2,1)S(1)}, u32[]{:S(2)}, u32[]{:S(2)}) collective-permute-start(bf16[2,128,640]{2,1,0:T(8,128)(2,1)S(1)} %shard_map.79), channel_id=1, source_target_pairs={{0,64},{1,65},{2,66},{3,67},{4,68},{5,69},{6,70},{7,71},{8,72},{9,... | collective-permute-start | bytes 983048 | tf_op jit(solution)/shard_map/ppermute | solution.py:360

commit v3 on v2

--- a/solution.py
+++ b/solution.py
@@ -65,8 +65,8 @@
     return jnp.repeat(bias, BLK, axis=2)
 
 
-def pack_kernel(at_ref, q_ref, k_ref, v_ref, out0, out1, out2, out3, sems):
-    me = at_ref[0]
+def pack_kernel(q_ref, k_ref, v_ref, out0, out1, out2, out3, sems):
+    me = lax.axis_index("frame") % GROUP
     outs = (out0, out1, out2, out3)
     width = out0.shape[2]
     copies = []
@@ -147,54 +147,60 @@
     )(place, low, high, after)
 
 
-def corner_kernel(own_pair, at_ref, *refs):
+def corner_kernel(
+    at_ref, low_own, high_own, second, low_oth, high_oth, direct, out_own, out_oth, sems
+):
     me, x_at = at_ref[0], at_ref[1]
-    out, sems = refs[-2], refs[-1]
-    lows, highs = refs[: (len(refs) - 2) // 2], refs[(len(refs) - 2) // 2 : -2]
-    length = lows[0].shape[2]
-    if own_pair:
-        slot = jnp.where(me < 2, me, 3 - me)
-    else:
-        slot = jnp.where(me < 2, 1 - me, me - 2)
-
-    def from_low(source):
+    length = low_own.shape[2]
+    own = (jnp.where(me < 2, me, 3 - me), out_own, 0)
+    oth = (jnp.where(me < 2, 1 - me, me - 2), out_oth, 2)
+
+    def from_low(source, slot, out, sem):
         rows = pl.ds(length - BLK, BLK)
-        return pltpu.make_async_copy(source.at[slot, :, rows], out.at[:, pl.ds(0, BLK)], sems.at[0])
-
-    def from_high(source):
+        return pltpu.make_async_copy(source.at[slot, :, rows], out.at[:, pl.ds(0, BLK)], sems.at[sem])
+
+    def from_high(source, slot, out, sem):
         rows = pl.ds(0, BLK)
-        return pltpu.make_async_copy(source.at[slot, :, rows], out.at[:, pl.ds(BLK, BLK)], sems.at[1])
+        return pltpu.make_async_copy(
+            source.at[slot, :, rows], out.at[:, pl.ds(BLK, BLK)], sems.at[sem + 1]
+        )
 
     @pl.when(x_at == 0)
     def _():
-        from_low(lows[1]).start()
+        from_low(second, *own).start()
+        from_low(direct, *oth).start()
 
     @pl.when(x_at != 0)
     def _():
-        from_low(lows[0]).start()
+        from_low(low_own, *own).start()
+        from_low(low_oth, *oth).start()
 
     @pl.when(x_at == XN - 1)
     def _():
-        from_high(highs[1]).start()
+        from_high(second, *own).start()
+        from_high(direct, *oth).start()
 
     @pl.when(x_at != XN - 1)
     def _():
-        from_high(highs[0]).start()
-
-    from_low(lows[0]).wait()
-    from_high(highs[0]).wait()
-
-
-def corner(own_pair, place, lows, highs):
-    shape = lows[0].shape
+        from_high(high_own, *own).start()
+        from_high(high_oth, *oth).start()
+
+    from_low(low_own, *own).wait()
+    from_high(high_own, *own).wait()
+    from_low(low_oth, *oth).wait()
+    from_high(high_oth, *oth).wait()
+
+
+def corners_of(place, *arrays):
+    shape = jax.ShapeDtypeStruct((2, 2 * BLK, arrays[0].shape[3]), jnp.bfloat16)
     return pl.pallas_call(
-        functools.partial(corner_kernel, own_pair),
-        in_specs=[SMEM] + [ANY] * (len(lows) + len(highs)),
-        out_specs=VMEM,
-        out_shape=jax.ShapeDtypeStruct((2, 2 * BLK, shape[3]), jnp.bfloat16),
-        scratch_shapes=[pltpu.SemaphoreType.DMA((2,))],
+        corner_kernel,
+        in_specs=[SMEM] + [ANY] * len(arrays),
+        out_specs=[VMEM] * 2,
+        out_shape=[shape] * 2,
+        scratch_shapes=[pltpu.SemaphoreType.DMA((4,))],
         compiler_params=pltpu.CompilerParams(vmem_limit_bytes=4 * 2**20),
-    )(place, *lows, *highs)
+    )(place, *arrays)
 
 
 def head_scores(query, keys, bias):
@@ -361,12 +367,12 @@
 
     packed = pl.pallas_call(
         pack_kernel,
-        in_specs=[SMEM] + [ANY] * 3,
+        in_specs=[ANY] * 3,
         out_specs=[VMEM] * GROUP,
         out_shape=[jax.ShapeDtypeStruct((3, length, part), jnp.bfloat16)] * GROUP,
         scratch_shapes=[pltpu.SemaphoreType.DMA((GROUP, 3))],
         compiler_params=pltpu.CompilerParams(vmem_limit_bytes=56 * 2**20),
-    )(place, queries[0], key_states[0], value_states[0])
+    )(queries[0], key_states[0], value_states[0])
 
     def flip(bits):
         return lambda f, r: (f ^ bits, r)
@@ -412,8 +418,7 @@
     later = join(arrived[2], arrived[3], partial[0])
     low_oth, high_oth = send(later, row_inner(1)), send(later, row_inner(-1))
     z_oth = send(later, z_target(False))
-    c_own = corner(True, place, [low_own, second], [high_own, second])
-    c_oth = corner(False, place, [low_oth, direct], [high_oth, direct])
+    c_own, c_oth = corners_of(place, low_own, high_own, second, low_oth, high_oth, direct)
     c_own, c_oth = send(c_own, z_target(True)), send(c_oth, z_target(False))
 
     arrays = arrived + list(partial) + [low_own, high_own, second, low_oth, high_oth, direct]

time: 109 us -> 107 us (0.982)
  Pallas kernels: 18.5 us -> 17.3 us
    pallas_call x3 -> x2, Pallas kernels: 5.25 us -> 4.05 us  [the longest x1 3.02 us: shards(): pl.pallas_call(pack_kernel, in_specs=[ANY] * 3, out_specs=[VMEM] * GROUP,...]
  transfers between devices with their start and end apart: 13 -> 13, of which waited for: 4 -> 5; matrix products, arithmetic and copies ran while one was open for 4% -> 4% of each run, Pallas kernels for 9% -> 9%
where the time goes in v3:
time: 107 us
  starting transfers between devices  38.8 us (36%)
  waiting for transfers between devices  28.7 us (27%)
  Pallas kernels  17.3 us (16%)
  blocking collectives  17.1 us (16%)
  local copies, waits for them, and re-layouts  3.21 us (3%)
  other arithmetic  1.28 us (1%)
    ppermute x13, starting transfers between devices, send(): return lax.ppermute(array, AXES, pairs_of(frame_total, row_total, target))  38.8 us
    ppermute x13, waiting for transfers between devices, send(): return lax.ppermute(array, AXES, pairs_of(frame_total, row_total, target))  28.7 us
    all_to_all x1, blocking collectives, shards(): back = lax.all_to_all(by_frame, 'frame', 0, 0, axis_index_groups=groups)  17.1 us
    pallas_call x3, Pallas kernels, attend(): pl.pallas_call(kernel, in_specs=[SMEM] + [VMEM] * (1 + len(arrays)) + [AN...  11.2 us
    pallas_call x1, Pallas kernels, shards(): pl.pallas_call(pack_kernel, in_specs=[ANY] * 3, out_specs=[VMEM] * GROUP,...  3.02 us
  transfers between devices with their start and end apart: 13, of which 5 were waited for; matrix products, arithmetic and copies ran while one was open for 4% of the time, Pallas kernels for 9%

profile of v3, /device:TPU:240, one launch (start us, length us, event | category | flops | bytes accessed | tf_op | source)
XLA Modules:
  0.0 106.8 jit_solution(14607774967251659325)
XLA Ops:
  0.0 3.0 %shard_map.73 = (bf16[3,128,640]{2,1,0:T(8,128)(2,1)}, bf16[3,128,640]{2,1,0:T(8,128)(2,1)}, bf16[3,128,640]{2,1,0:T(8,128)(2,1)}, bf16[3,128,640]{2,1,0:T(8,128)(2,1)}) custom-call(bf16[128,2560]{1,0:T(8,128)(2,1)} %bitcast.10, bf16[128,2560]{1,0:T(8,128)(2,1)} %bitcast.11, bf16[128,2560]{1,0:T(8,128)(2,1)} %bitcast.12), custom_call_target="tpu_custom_call" | custom-call | tf_op jit(solution)/shard_map/pallas_call | solution.py:368
  3.0 1.9 %collective-permute-start = (bf16[3,128,640]{2,1,0:T(8,128)(2,1)}, bf16[3,128,640]{2,1,0:T(8,128)(2,1)S(1)}, u32[]{:S(2)}, u32[]{:S(2)}) collective-permute-start(bf16[3,128,640]{2,1,0:T(8,128)(2,1)} %get-tuple-element.15), channel_id=1, source_target_pairs={{0,16},{1,17},{2,18},{3,19},{4,20},{5,21},{6,22},{7,23},{8,24},{9,... | collective-permute-start | bytes 1474568 | tf_op jit(solution)/shard_map/ppermute | solution.py:366
  5.0 2.6 %collective-permute-start.1 = (bf16[3,128,640]{2,1,0:T(8,128)(2,1)}, bf16[3,128,640]{2,1,0:T(8,128)(2,1)S(1)}, u32[]{:S(2)}, u32[]{:S(2)}) collective-permute-start(bf16[3,128,640]{2,1,0:T(8,128)(2,1)} %get-tuple-element.16), channel_id=1, source_target_pairs={{0,32},{1,33},{2,34},{3,35},{4,36},{5,37},{6,38},{7,39},{8,40},{9,... | collective-permute-start | bytes 1474568 | tf_op jit(solution)/shard_map/ppermute | solution.py:366
  7.6 3.1 %collective-permute-start.2 = (bf16[3,128,640]{2,1,0:T(8,128)(2,1)}, bf16[3,128,640]{2,1,0:T(8,128)(2,1)S(1)}, u32[]{:S(2)}, u32[]{:S(2)}) collective-permute-start(bf16[3,128,640]{2,1,0:T(8,128)(2,1)} %get-tuple-element.17), channel_id=1, source_target_pairs={{0,48},{1,49},{2,50},{3,51},{4,52},{5,53},{6,54},{7,55},{8,56},{9,... | collective-permute-start | bytes 1474568 | tf_op jit(solution)/shard_map/ppermute | solution.py:366
  11.1 1.0 slice_bitcast_fusion.1
  12.2 0.9 pad_maximum_fusion.own
  13.1 3.4 %collective-permute-start.3 = (bf16[2,2,128,640]{3,2,1,0:T(8,128)(2,1)}, bf16[2,2,128,640]{3,2,1,0:T(8,128)(2,1)S(1)}, u32[]{:S(2)}, u32[]{:S(2)}) collective-permute-start(bf16[2,2,128,640]{3,2,1,0:T(8,128)(2,1)} %pad_maximum_fusion.own), channel_id=1, source_target_pairs={{0,1},{1,2},{2,3},{3,0},{4,5},{5,6},{6,7},{7,4},{8,9},{9,10},{10,1... | collective-permute-start | bytes 1966088 | tf_op jit(solution)/shard_map/ppermute | solution.py:366
  16.5 3.7 %collective-permute-start.4 = (bf16[2,2,128,640]{3,2,1,0:T(8,128)(2,1)}, bf16[2,2,128,640]{3,2,1,0:T(8,128)(2,1)S(1)}, u32[]{:S(2)}, u32[]{:S(2)}) collective-permute-start(bf16[2,2,128,640]{3,2,1,0:T(8,128)(2,1)} %pad_maximum_fusion.own), channel_id=1, source_target_pairs={{0,3},{1,0},{2,1},{3,2},{4,7},{5,4},{6,5},{7,6},{8,11},{9,8},{10,9... | collective-permute-start | bytes 1966088 | tf_op jit(solution)/shard_map/ppermute | solution.py:366
  20.1 1.9 %collective-permute-start.5 = (bf16[2,2,128,640]{3,2,1,0:T(8,128)(2,1)}, bf16[2,2,128,640]{3,2,1,0:T(8,128)(2,1)S(1)}, u32[]{:S(2)}, u32[]{:S(2)}) collective-permute-start(bf16[2,2,128,640]{3,2,1,0:T(8,128)(2,1)} %pad_maximum_fusion.own), channel_id=1, source_target_pairs={{32,96},{33,97},{34,98},{35,99},{36,100},{37,101},{38,102},{39,103... | collective-permute-start | bytes 1966088 | tf_op jit(solution)/shard_map/ppermute | solution.py:366
  22.3 0.7 broadcast_in_dim.21
  23.0 1.0 reshape.59.bias_ref
  24.1 6.7 %collective-permute-done.2.second.got3 = bf16[3,128,640]{2,1,0:T(8,128)(2,1)S(1)} collective-permute-done((bf16[3,128,640]{2,1,0:T(8,128)(2,1)}, bf16[3,128,640]{2,1,0:T(8,128)(2,1)S(1)}, u32[]{:S(2)}, u32[]{:S(2)}) %collective-permute-start.2) | collective-permute-done | bytes 491552 | tf_op jit(solution)/shard_map/ppermute | solution.py:366
  30.8 0.2 shard_map.74.after.oth
  31.1 6.4 %collective-permute-start.9 = (bf16[2,2,128,640]{3,2,1,0:T(8,128)(2,1)S(1)}, bf16[2,2,128,640]{3,2,1,0:T(8,128)(2,1)S(1)}, u32[]{:S(2)}, u32[]{:S(2)}) collective-permute-start(bf16[2,2,128,640]{3,2,1,0:T(8,128)(2,1)S(1)} %shard_map.74.after.oth), channel_id=1, source_target_pairs={{3,4},{4,3},{7,8},{8,7},{11,12},{12,11},{19,20},{20,19},{23,24},{2... | collective-permute-start | bytes 1966088 | tf_op jit(solution)/shard_map/ppermute | solution.py:366
  37.5 0.8 shard_map.75.after0
  38.2 1.3 %collective-permute-start.6 = (bf16[2,2,128,640]{3,2,1,0:T(8,128)(2,1)S(1)}, bf16[2,2,128,640]{3,2,1,0:T(8,128)(2,1)S(1)}, u32[]{:S(2)}, u32[]{:S(2)}) collective-permute-start(bf16[2,2,128,640]{3,2,1,0:T(8,128)(2,1)S(1)} %shard_map.75.after0), channel_id=1, source_target_pairs={{0,4},{4,8},{7,3},{8,12},{11,7},{15,11},{16,20},{20,24},{23,19},{2... | collective-permute-start | bytes 1966088 | tf_op jit(solution)/shard_map/ppermute | solution.py:366
  39.5 0.9 collective-permute-done.5.after1.z_own
  40.5 4.0 %shard_map.76 = (f32[4,128,640]{2,1,0:T(8,128)S(1)}, f32[4,128,640]{2,1,0:T(8,128)S(1)}, f32[4,128,640]{2,1,0:T(8,128)S(1)}) custom-call(s32[2]{0:T(128)S(1)} %pad_add_fusion.at_ref, f32[4,2,1152]{2,1,0:T(2,128)S(1)} %reshape.59.bias_ref, bf16[3,128,640]{2,1,0:T(8,128)(2,1)S(1)} %copy-done.1, bf16[3,128,640]{2,1,0:T(8,128)(2,1)S(1)} %collective-permute-done.got1, ...), custom_call_target="tpu_custom_call" | custom-call | flops 587202560 | bytes 8000000 | tf_op jit(solution)/shard_map/pallas_call | solution.py:342
  44.5 0.2 shard_map.77
  44.7 2.2 %collective-permute-start.7 = (bf16[2,2,128,640]{3,2,1,0:T(8,128)(2,1)S(1)}, bf16[2,2,128,640]{3,2,1,0:T(8,128)(2,1)S(1)}, u32[]{:S(2)}, u32[]{:S(2)}) collective-permute-start(bf16[2,2,128,640]{3,2,1,0:T(8,128)(2,1)S(1)} %shard_map.77), channel_id=1, source_target_pairs={{0,1},{1,2},{2,3},{4,5},{5,6},{6,7},{8,9},{9,10},{10,11},{12,13},{... | collective-permute-start | bytes 1966088 | tf_op jit(solution)/shard_map/ppermute | solution.py:366
  47.0 1.3 %collective-permute-start.8 = (bf16[2,2,128,640]{3,2,1,0:T(8,128)(2,1)S(1)}, bf16[2,2,128,640]{3,2,1,0:T(8,128)(2,1)S(1)}, u32[]{:S(2)}, u32[]{:S(2)}) collective-permute-start(bf16[2,2,128,640]{3,2,1,0:T(8,128)(2,1)S(1)} %shard_map.77), channel_id=1, source_target_pairs={{1,0},{2,1},{3,2},{5,4},{6,5},{7,6},{9,8},{10,9},{11,10},{13,12},{... | collective-permute-start | bytes 1966088 | tf_op jit(solution)/shard_map/ppermute | solution.py:366
  48.3 3.7 %collective-permute-start.10 = (bf16[2,2,128,640]{3,2,1,0:T(8,128)(2,1)S(1)}, bf16[2,2,128,640]{3,2,1,0:T(8,128)(2,1)S(1)}, u32[]{:S(2)}, u32[]{:S(2)}) collective-permute-start(bf16[2,2,128,640]{3,2,1,0:T(8,128)(2,1)S(1)} %shard_map.77), channel_id=1, source_target_pairs={{0,64},{1,65},{2,66},{3,67},{4,68},{5,69},{6,70},{7,71},{8,72},{9,... | collective-permute-start | bytes 1966088 | tf_op jit(solution)/shard_map/ppermute | solution.py:366
  52.0 14.2 %collective-permute-done.9.direct = bf16[2,2,128,640]{3,2,1,0:T(8,128)(2,1)S(1)} collective-permute-done((bf16[2,2,128,640]{3,2,1,0:T(8,128)(2,1)S(1)}, bf16[2,2,128,640]{3,2,1,0:T(8,128)(2,1)S(1)}, u32[]{:S(2)}, u32[]{:S(2)}) %collective-permute-start.9) | collective-permute-done | bytes 655392 | tf_op jit(solution)/shard_map/ppermute | solution.py:366
  66.1 5.9 %collective-permute-done.6.second = bf16[2,2,128,640]{3,2,1,0:T(8,128)(2,1)S(1)} collective-permute-done((bf16[2,2,128,640]{3,2,1,0:T(8,128)(2,1)S(1)}, bf16[2,2,128,640]{3,2,1,0:T(8,128)(2,1)S(1)}, u32[]{:S(2)}, u32[]{:S(2)}) %collective-permute-start.6) | collective-permute-done | bytes 655392 | tf_op jit(solution)/shard_map/ppermute | solution.py:366
  72.0 1.0 shard_map.78
  73.0 1.9 %collective-permute-start.11 = (bf16[2,128,640]{2,1,0:T(8,128)(2,1)S(1)}, bf16[2,128,640]{2,1,0:T(8,128)(2,1)S(1)}, u32[]{:S(2)}, u32[]{:S(2)}) collective-permute-start(bf16[2,128,640]{2,1,0:T(8,128)(2,1)S(1)} %get-tuple-element.21), channel_id=1, source_target_pairs={{32,96},{33,97},{34,98},{35,99},{36,100},{37,101},{38,102},{39,103... | collective-permute-start | bytes 983048 | tf_op jit(solution)/shard_map/ppermute | solution.py:366
  75.0 5.5 %collective-permute-start.12 = (bf16[2,128,640]{2,1,0:T(8,128)(2,1)S(1)}, bf16[2,128,640]{2,1,0:T(8,128)(2,1)S(1)}, u32[]{:S(2)}, u32[]{:S(2)}) collective-permute-start(bf16[2,128,640]{2,1,0:T(8,128)(2,1)S(1)} %get-tuple-element.22), channel_id=1, source_target_pairs={{0,64},{1,65},{2,66},{3,67},{4,68},{5,69},{6,70},{7,71},{8,72},{9,... | collective-permute-start | bytes 983048 | tf_op jit(solution)/shard_map/ppermute | solution.py:366
  80.5 3.5 %shard_map.80 = bf16[2,128,640]{2,1,0:T(8,128)(2,1)S(1)} custom-call(s32[2]{0:T(128)S(1)} %pad_add_fusion.at_ref, f32[4,2,1152]{2,1,0:T(2,128)S(1)} %reshape.59.bias_ref, bf16[3,128,640]{2,1,0:T(8,128)(2,1)S(1)} %copy-done.1, bf16[3,128,640]{2,1,0:T(8,128)(2,1)S(1)} %collective-permute-done.got1, bf16[3,128,640]{2,1,0:T(8,128)(2,1)S(1)} %collective-permute-done.1.first.got2, ...), custom_call_target="tpu_custom_call" | custom-call | flops 335544320 | bytes 8000000 | tf_op jit(solution)/shard_map/pallas_call | solution.py:342
  84.0 1.1 collective-permute-done.12.rest_1_
  85.0 3.7 %shard_map.79 = bf16[2,128,640]{2,1,0:T(8,128)(2,1)S(1)} custom-call(s32[2]{0:T(128)S(1)} %pad_add_fusion.at_ref, f32[4,2,1152]{2,1,0:T(2,128)S(1)} %reshape.59.bias_ref, bf16[3,128,640]{2,1,0:T(8,128)(2,1)S(1)} %copy-done.1, bf16[3,128,640]{2,1,0:T(8,128)(2,1)S(1)} %collective-permute-done.got1, bf16[3,128,640]{2,1,0:T(8,128)(2,1)S(1)} %collective-permute-done.1.first.got2, ...), custom_call_target="tpu_custom_call" | custom-call | flops 335544320 | bytes 8000000 | tf_op jit(solution)/shard_map/pallas_call | solution.py:342
  88.8 17.1 %all_to_all.5.in_ref = bf16[4,128,640]{2,1,0:T(8,128)(2,1)S(1)} all-to-all(bf16[4,128,640]{2,1,0:T(8,128)(2,1)S(1)} %pad_maximum_fusion.1), channel_id=1, replica_groups={{0,16,32,48},{64,80,96,112},{128,144,160,176},{192,208,224,240},{256,27..., dimensions={0} | all-to-all | bytes 1310720 | tf_op jit(solution)/shard_map/all_to_all | solution.py:437
  105.9 0.9 shard_map.81
  (34 shorter events, 0.9 us)
Async XLA Ops:
  0.0 10.7 %copy-start = (s32[5,32,5]{1,2,0:T(8,128)S(1)}, s32[5,32,5]{1,2,0:T(8,128)}, u32[]{:S(2)}) copy-start(s32[5,32,5]{1,2,0:T(8,128)} %param.10) | copy-start | bytes 9604
  0.0 10.7 %copy-start.4 = (s32[18]{0:T(128)S(1)}, s32[18]{0:T(128)}, u32[]{:S(2)}) copy-start(s32[18]{0:T(128)} %constant.48.clone) | copy-start | bytes 220
  0.0 11.0 %copy-start.3 = (s32[18]{0:T(128)S(1)}, s32[18]{0:T(128)}, u32[]{:S(2)}) copy-start(s32[18]{0:T(128)} %constant.47.clone) | copy-start | bytes 220
  3.0 9.1 %collective-permute-start = (bf16[3,128,640]{2,1,0:T(8,128)(2,1)}, bf16[3,128,640]{2,1,0:T(8,128)(2,1)S(1)}, u32[]{:S(2)}, u32[]{:S(2)}) collective-permute-start(bf16[3,128,640]{2,1,0:T(8,128)(2,1)} %get-tuple-element.15), channel_id=1, source_target_pairs={{0,16},{1,17},{2,18},{3,19},{4,20},{5,21},{6,22},{7,23},{8,24},{9,... | collective-permute-start | bytes 1474568 | tf_op jit(solution)/shard_map/ppermute | solution.py:366
  5.0 19.1 %collective-permute-start.1 = (bf16[3,128,640]{2,1,0:T(8,128)(2,1)}, bf16[3,128,640]{2,1,0:T(8,128)(2,1)S(1)}, u32[]{:S(2)}, u32[]{:S(2)}) collective-permute-start(bf16[3,128,640]{2,1,0:T(8,128)(2,1)} %get-tuple-element.16), channel_id=1, source_target_pairs={{0,32},{1,33},{2,34},{3,35},{4,36},{5,37},{6,38},{7,39},{8,40},{9,... | collective-permute-start | bytes 1474568 | tf_op jit(solution)/shard_map/ppermute | solution.py:366
  7.6 23.3 %collective-permute-start.2 = (bf16[3,128,640]{2,1,0:T(8,128)(2,1)}, bf16[3,128,640]{2,1,0:T(8,128)(2,1)S(1)}, u32[]{:S(2)}, u32[]{:S(2)}) collective-permute-start(bf16[3,128,640]{2,1,0:T(8,128)(2,1)} %get-tuple-element.17), channel_id=1, source_target_pairs={{0,48},{1,49},{2,50},{3,51},{4,52},{5,53},{6,54},{7,55},{8,56},{9,... | collective-permute-start | bytes 1474568 | tf_op jit(solution)/shard_map/ppermute | solution.py:366
  11.1 11.0 %copy-start.2 = (f32[2,18,50]{2,0,1:T(2,128)S(1)}, f32[2,18,50]{2,0,1:T(2,128)}, u32[]{:S(2)}) copy-start(f32[2,18,50]{2,0,1:T(2,128)} %constant.46.clone) | copy-start | bytes 21604
  13.1 24.4 %collective-permute-start.3 = (bf16[2,2,128,640]{3,2,1,0:T(8,128)(2,1)}, bf16[2,2,128,640]{3,2,1,0:T(8,128)(2,1)S(1)}, u32[]{:S(2)}, u32[]{:S(2)}) collective-permute-start(bf16[2,2,128,640]{3,2,1,0:T(8,128)(2,1)} %pad_maximum_fusion.own), channel_id=1, source_target_pairs={{0,1},{1,2},{2,3},{3,0},{4,5},{5,6},{6,7},{7,4},{8,9},{9,10},{10,1... | collective-permute-start | bytes 1966088 | tf_op jit(solution)/shard_map/ppermute | solution.py:366
  16.5 21.0 %collective-permute-start.4 = (bf16[2,2,128,640]{3,2,1,0:T(8,128)(2,1)}, bf16[2,2,128,640]{3,2,1,0:T(8,128)(2,1)S(1)}, u32[]{:S(2)}, u32[]{:S(2)}) collective-permute-start(bf16[2,2,128,640]{3,2,1,0:T(8,128)(2,1)} %pad_maximum_fusion.own), channel_id=1, source_target_pairs={{0,3},{1,0},{2,1},{3,2},{4,7},{5,4},{6,5},{7,6},{8,11},{9,8},{10,9... | collective-permute-start | bytes 1966088 | tf_op jit(solution)/shard_map/ppermute | solution.py:366
  20.1 20.3 %collective-permute-start.5 = (bf16[2,2,128,640]{3,2,1,0:T(8,128)(2,1)}, bf16[2,2,128,640]{3,2,1,0:T(8,128)(2,1)S(1)}, u32[]{:S(2)}, u32[]{:S(2)}) collective-permute-start(bf16[2,2,128,640]{3,2,1,0:T(8,128)(2,1)} %pad_maximum_fusion.own), channel_id=1, source_target_pairs={{32,96},{33,97},{34,98},{35,99},{36,100},{37,101},{38,102},{39,103... | collective-permute-start | bytes 1966088 | tf_op jit(solution)/shard_map/ppermute | solution.py:366
  31.1 9.4 %copy-start.1 = (bf16[3,128,640]{2,1,0:T(8,128)(2,1)S(1)}, bf16[3,128,640]{2,1,0:T(8,128)(2,1)}, u32[]{:S(2)}) copy-start(bf16[3,128,640]{2,1,0:T(8,128)(2,1)} %get-tuple-element.14.got0) | copy-start | bytes 1474564
  31.1 35.1 %collective-permute-start.9 = (bf16[2,2,128,640]{3,2,1,0:T(8,128)(2,1)S(1)}, bf16[2,2,128,640]{3,2,1,0:T(8,128)(2,1)S(1)}, u32[]{:S(2)}, u32[]{:S(2)}) collective-permute-start(bf16[2,2,128,640]{3,2,1,0:T(8,128)(2,1)S(1)} %shard_map.74.after.oth), channel_id=1, source_target_pairs={{3,4},{4,3},{7,8},{8,7},{11,12},{12,11},{19,20},{20,19},{23,24},{2... | collective-permute-start | bytes 1966088 | tf_op jit(solution)/shard_map/ppermute | solution.py:366
  38.2 33.8 %collective-permute-start.6 = (bf16[2,2,128,640]{3,2,1,0:T(8,128)(2,1)S(1)}, bf16[2,2,128,640]{3,2,1,0:T(8,128)(2,1)S(1)}, u32[]{:S(2)}, u32[]{:S(2)}) collective-permute-start(bf16[2,2,128,640]{3,2,1,0:T(8,128)(2,1)S(1)} %shard_map.75.after0), channel_id=1, source_target_pairs={{0,4},{4,8},{7,3},{8,12},{11,7},{15,11},{16,20},{20,24},{23,19},{2... | collective-permute-start | bytes 1966088 | tf_op jit(solution)/shard_map/ppermute | solution.py:366
  44.7 27.3 %collective-permute-start.7 = (bf16[2,2,128,640]{3,2,1,0:T(8,128)(2,1)S(1)}, bf16[2,2,128,640]{3,2,1,0:T(8,128)(2,1)S(1)}, u32[]{:S(2)}, u32[]{:S(2)}) collective-permute-start(bf16[2,2,128,640]{3,2,1,0:T(8,128)(2,1)S(1)} %shard_map.77), channel_id=1, source_target_pairs={{0,1},{1,2},{2,3},{4,5},{5,6},{6,7},{8,9},{9,10},{10,11},{12,13},{... | collective-permute-start | bytes 1966088 | tf_op jit(solution)/shard_map/ppermute | solution.py:366
  47.0 25.0 %collective-permute-start.8 = (bf16[2,2,128,640]{3,2,1,0:T(8,128)(2,1)S(1)}, bf16[2,2,128,640]{3,2,1,0:T(8,128)(2,1)S(1)}, u32[]{:S(2)}, u32[]{:S(2)}) collective-permute-start(bf16[2,2,128,640]{3,2,1,0:T(8,128)(2,1)S(1)} %shard_map.77), channel_id=1, source_target_pairs={{1,0},{2,1},{3,2},{5,4},{6,5},{7,6},{9,8},{10,9},{11,10},{13,12},{... | collective-permute-start | bytes 1966088 | tf_op jit(solution)/shard_map/ppermute | solution.py:366
  48.3 32.2 %collective-permute-start.10 = (bf16[2,2,128,640]{3,2,1,0:T(8,128)(2,1)S(1)}, bf16[2,2,128,640]{3,2,1,0:T(8,128)(2,1)S(1)}, u32[]{:S(2)}, u32[]{:S(2)}) collective-permute-start(bf16[2,2,128,640]{3,2,1,0:T(8,128)(2,1)S(1)} %shard_map.77), channel_id=1, source_target_pairs={{0,64},{1,65},{2,66},{3,67},{4,68},{5,69},{6,70},{7,71},{8,72},{9,... | collective-permute-start | bytes 1966088 | tf_op jit(solution)/shard_map/ppermute | solution.py:366
  73.0 10.9 %collective-permute-start.11 = (bf16[2,128,640]{2,1,0:T(8,128)(2,1)S(1)}, bf16[2,128,640]{2,1,0:T(8,128)(2,1)S(1)}, u32[]{:S(2)}, u32[]{:S(2)}) collective-permute-start(bf16[2,128,640]{2,1,0:T(8,128)(2,1)S(1)} %get-tuple-element.21), channel_id=1, source_target_pairs={{32,96},{33,97},{34,98},{35,99},{36,100},{37,101},{38,102},{39,103... | collective-permute-start | bytes 983048 | tf_op jit(solution)/shard_map/ppermute | solution.py:366
  75.0 10.1 %collective-permute-start.12 = (bf16[2,128,640]{2,1,0:T(8,128)(2,1)S(1)}, bf16[2,128,640]{2,1,0:T(8,128)(2,1)S(1)}, u32[]{:S(2)}, u32[]{:S(2)}) collective-permute-start(bf16[2,128,640]{2,1,0:T(8,128)(2,1)S(1)} %get-tuple-element.22), channel_id=1, source_target_pairs={{0,64},{1,65},{2,66},{3,67},{4,68},{5,69},{6,70},{7,71},{8,72},{9,... | collective-permute-start | bytes 983048 | tf_op jit(solution)/shard_map/ppermute | solution.py:366

commit v4 on v3

--- a/solution.py
+++ b/solution.py
@@ -379,7 +379,7 @@
 
     groups = [list(range(f, f + GROUP)) for f in range(0, frame_total, GROUP)]
     arrived = [packed[0]] + [send(packed[s], flip(s)) for s in range(1, GROUP)]
-    own = jnp.stack([arrived[0][:2], arrived[1][:2]])
+    own = join(arrived[0], arrived[1])
 
     def row_first(by):
         edge = XN - 1 if by > 0 else 0

time: 107 us -> 107 us (level)
  Pallas kernels: 17.3 us -> 18.4 us
  transfers between devices with their start and end apart: 13 -> 13, of which waited for: 5 -> 5; matrix products, arithmetic and copies ran while one was open for 4% -> 2% of each run, Pallas kernels for 9% -> 10%
where the time goes in v4:
time: 107 us
  starting transfers between devices  38.8 us (36%)
  waiting for transfers between devices  28.7 us (27%)
  Pallas kernels  18.4 us (17%)
  blocking collectives  17.1 us (16%)
  local copies, waits for them, and re-layouts  3.19 us (3%)
    ppermute x13, starting transfers between devices, send(): return lax.ppermute(array, AXES, pairs_of(frame_total, row_total, target))  38.8 us
    ppermute x13, waiting for transfers between devices, send(): return lax.ppermute(array, AXES, pairs_of(frame_total, row_total, target))  28.7 us
    all_to_all x1, blocking collectives, shards(): back = lax.all_to_all(by_frame, 'frame', 0, 0, axis_index_groups=groups)  17.1 us
    pallas_call x3, Pallas kernels, attend(): pl.pallas_call(kernel, in_specs=[SMEM] + [VMEM] * (1 + len(arrays)) + [AN...  11.2 us
    pallas_call x1, Pallas kernels, shards(): pl.pallas_call(pack_kernel, in_specs=[ANY] * 3, out_specs=[VMEM] * GROUP,...  3.04 us
  transfers between devices with their start and end apart: 13, of which 5 were waited for; matrix products, arithmetic and copies ran while one was open for 2% of the time, Pallas kernels for 10%

profile of v4, /device:TPU:240, one launch (start us, length us, event | category | flops | bytes accessed | tf_op | source)
XLA Modules:
  0.0 106.8 jit_solution(8432734208149509676)
XLA Ops:
  0.0 3.0 %shard_map.73 = (bf16[3,128,640]{2,1,0:T(8,128)(2,1)}, bf16[3,128,640]{2,1,0:T(8,128)(2,1)}, bf16[3,128,640]{2,1,0:T(8,128)(2,1)}, bf16[3,128,640]{2,1,0:T(8,128)(2,1)}) custom-call(bf16[128,2560]{1,0:T(8,128)(2,1)} %bitcast.6, bf16[128,2560]{1,0:T(8,128)(2,1)} %bitcast.7, bf16[128,2560]{1,0:T(8,128)(2,1)} %bitcast.8), custom_call_target="tpu_custom_call" | custom-call | tf_op jit(solution)/shard_map/pallas_call | solution.py:368
  3.1 1.9 %collective-permute-start = (bf16[3,128,640]{2,1,0:T(8,128)(2,1)}, bf16[3,128,640]{2,1,0:T(8,128)(2,1)S(1)}, u32[]{:S(2)}, u32[]{:S(2)}) collective-permute-start(bf16[3,128,640]{2,1,0:T(8,128)(2,1)} %get-tuple-element.15), channel_id=1, source_target_pairs={{0,16},{1,17},{2,18},{3,19},{4,20},{5,21},{6,22},{7,23},{8,24},{9,... | collective-permute-start | bytes 1474568 | tf_op jit(solution)/shard_map/ppermute | solution.py:366
  5.0 2.6 %collective-permute-start.1 = (bf16[3,128,640]{2,1,0:T(8,128)(2,1)}, bf16[3,128,640]{2,1,0:T(8,128)(2,1)S(1)}, u32[]{:S(2)}, u32[]{:S(2)}) collective-permute-start(bf16[3,128,640]{2,1,0:T(8,128)(2,1)} %get-tuple-element.16), channel_id=1, source_target_pairs={{0,32},{1,33},{2,34},{3,35},{4,36},{5,37},{6,38},{7,39},{8,40},{9,... | collective-permute-start | bytes 1474568 | tf_op jit(solution)/shard_map/ppermute | solution.py:366
  7.6 3.1 %collective-permute-start.2 = (bf16[3,128,640]{2,1,0:T(8,128)(2,1)}, bf16[3,128,640]{2,1,0:T(8,128)(2,1)S(1)}, u32[]{:S(2)}, u32[]{:S(2)}) collective-permute-start(bf16[3,128,640]{2,1,0:T(8,128)(2,1)} %get-tuple-element.17), channel_id=1, source_target_pairs={{0,48},{1,49},{2,50},{3,51},{4,52},{5,53},{6,54},{7,55},{8,56},{9,... | collective-permute-start | bytes 1474568 | tf_op jit(solution)/shard_map/ppermute | solution.py:366
  11.1 1.0 copy-done.1
  12.2 1.1 shard_map.74.own
  13.2 3.4 %collective-permute-start.3 = (bf16[2,2,128,640]{3,2,1,0:T(8,128)(2,1)}, bf16[2,2,128,640]{3,2,1,0:T(8,128)(2,1)S(1)}, u32[]{:S(2)}, u32[]{:S(2)}) collective-permute-start(bf16[2,2,128,640]{3,2,1,0:T(8,128)(2,1)} %shard_map.74.own), channel_id=1, source_target_pairs={{0,1},{1,2},{2,3},{3,0},{4,5},{5,6},{6,7},{7,4},{8,9},{9,10},{10,1... | collective-permute-start | bytes 1966088 | tf_op jit(solution)/shard_map/ppermute | solution.py:366
  16.6 3.7 %collective-permute-start.4 = (bf16[2,2,128,640]{3,2,1,0:T(8,128)(2,1)}, bf16[2,2,128,640]{3,2,1,0:T(8,128)(2,1)S(1)}, u32[]{:S(2)}, u32[]{:S(2)}) collective-permute-start(bf16[2,2,128,640]{3,2,1,0:T(8,128)(2,1)} %shard_map.74.own), channel_id=1, source_target_pairs={{0,3},{1,0},{2,1},{3,2},{4,7},{5,4},{6,5},{7,6},{8,11},{9,8},{10,9... | collective-permute-start | bytes 1966088 | tf_op jit(solution)/shard_map/ppermute | solution.py:366
  20.3 1.9 %collective-permute-start.5 = (bf16[2,2,128,640]{3,2,1,0:T(8,128)(2,1)}, bf16[2,2,128,640]{3,2,1,0:T(8,128)(2,1)S(1)}, u32[]{:S(2)}, u32[]{:S(2)}) collective-permute-start(bf16[2,2,128,640]{3,2,1,0:T(8,128)(2,1)} %shard_map.74.own), channel_id=1, source_target_pairs={{32,96},{33,97},{34,98},{35,99},{36,100},{37,101},{38,102},{39,103... | collective-permute-start | bytes 1966088 | tf_op jit(solution)/shard_map/ppermute | solution.py:366
  22.4 0.7 broadcast_in_dim.21
  23.2 1.0 reshape.59.bias_ref
  24.3 6.6 %collective-permute-done.2.second.got3 = bf16[3,128,640]{2,1,0:T(8,128)(2,1)S(1)} collective-permute-done((bf16[3,128,640]{2,1,0:T(8,128)(2,1)}, bf16[3,128,640]{2,1,0:T(8,128)(2,1)S(1)}, u32[]{:S(2)}, u32[]{:S(2)}) %collective-permute-start.2) | collective-permute-done | bytes 491552 | tf_op jit(solution)/shard_map/ppermute | solution.py:366
  30.9 0.2 shard_map.75.after.oth
  31.1 6.4 %collective-permute-start.9 = (bf16[2,2,128,640]{3,2,1,0:T(8,128)(2,1)S(1)}, bf16[2,2,128,640]{3,2,1,0:T(8,128)(2,1)S(1)}, u32[]{:S(2)}, u32[]{:S(2)}) collective-permute-start(bf16[2,2,128,640]{3,2,1,0:T(8,128)(2,1)S(1)} %shard_map.75.after.oth), channel_id=1, source_target_pairs={{3,4},{4,3},{7,8},{8,7},{11,12},{12,11},{19,20},{20,19},{23,24},{2... | collective-permute-start | bytes 1966088 | tf_op jit(solution)/shard_map/ppermute | solution.py:366
  37.5 0.8 shard_map.76.after0
  38.3 1.3 %collective-permute-start.6 = (bf16[2,2,128,640]{3,2,1,0:T(8,128)(2,1)S(1)}, bf16[2,2,128,640]{3,2,1,0:T(8,128)(2,1)S(1)}, u32[]{:S(2)}, u32[]{:S(2)}) collective-permute-start(bf16[2,2,128,640]{3,2,1,0:T(8,128)(2,1)S(1)} %shard_map.76.after0), channel_id=1, source_target_pairs={{0,4},{4,8},{7,3},{8,12},{11,7},{15,11},{16,20},{20,24},{23,19},{2... | collective-permute-start | bytes 1966088 | tf_op jit(solution)/shard_map/ppermute | solution.py:366
  39.6 1.0 collective-permute-done.5.after1.z_own
  40.6 4.0 %shard_map.77 = (f32[4,128,640]{2,1,0:T(8,128)S(1)}, f32[4,128,640]{2,1,0:T(8,128)S(1)}, f32[4,128,640]{2,1,0:T(8,128)S(1)}) custom-call(s32[2]{0:T(128)S(1)} %pad_add_fusion.at_ref, f32[4,2,1152]{2,1,0:T(2,128)S(1)} %reshape.59.bias_ref, bf16[3,128,640]{2,1,0:T(8,128)(2,1)S(1)} %copy-done.2, bf16[3,128,640]{2,1,0:T(8,128)(2,1)S(1)} %collective-permute-done.second.got1, ...), custom_call_target="tpu_custom_call" | custom-call | flops 587202560 | bytes 8000000 | tf_op jit(solution)/shard_map/pallas_call | solution.py:342
  44.7 0.2 shard_map.78
  44.9 2.2 %collective-permute-start.7 = (bf16[2,2,128,640]{3,2,1,0:T(8,128)(2,1)S(1)}, bf16[2,2,128,640]{3,2,1,0:T(8,128)(2,1)S(1)}, u32[]{:S(2)}, u32[]{:S(2)}) collective-permute-start(bf16[2,2,128,640]{3,2,1,0:T(8,128)(2,1)S(1)} %shard_map.78), channel_id=1, source_target_pairs={{0,1},{1,2},{2,3},{4,5},{5,6},{6,7},{8,9},{9,10},{10,11},{12,13},{... | collective-permute-start | bytes 1966088 | tf_op jit(solution)/shard_map/ppermute | solution.py:366
  47.1 1.3 %collective-permute-start.8 = (bf16[2,2,128,640]{3,2,1,0:T(8,128)(2,1)S(1)}, bf16[2,2,128,640]{3,2,1,0:T(8,128)(2,1)S(1)}, u32[]{:S(2)}, u32[]{:S(2)}) collective-permute-start(bf16[2,2,128,640]{3,2,1,0:T(8,128)(2,1)S(1)} %shard_map.78), channel_id=1, source_target_pairs={{1,0},{2,1},{3,2},{5,4},{6,5},{7,6},{9,8},{10,9},{11,10},{13,12},{... | collective-permute-start | bytes 1966088 | tf_op jit(solution)/shard_map/ppermute | solution.py:366
  48.4 3.6 %collective-permute-start.10 = (bf16[2,2,128,640]{3,2,1,0:T(8,128)(2,1)S(1)}, bf16[2,2,128,640]{3,2,1,0:T(8,128)(2,1)S(1)}, u32[]{:S(2)}, u32[]{:S(2)}) collective-permute-start(bf16[2,2,128,640]{3,2,1,0:T(8,128)(2,1)S(1)} %shard_map.78), channel_id=1, source_target_pairs={{0,64},{1,65},{2,66},{3,67},{4,68},{5,69},{6,70},{7,71},{8,72},{9,... | collective-permute-start | bytes 1966088 | tf_op jit(solution)/shard_map/ppermute | solution.py:366
  52.1 14.1 %collective-permute-done.9.direct = bf16[2,2,128,640]{3,2,1,0:T(8,128)(2,1)S(1)} collective-permute-done((bf16[2,2,128,640]{3,2,1,0:T(8,128)(2,1)S(1)}, bf16[2,2,128,640]{3,2,1,0:T(8,128)(2,1)S(1)}, u32[]{:S(2)}, u32[]{:S(2)}) %collective-permute-start.9) | collective-permute-done | bytes 655392 | tf_op jit(solution)/shard_map/ppermute | solution.py:366
  66.2 5.9 %collective-permute-done.6.second = bf16[2,2,128,640]{3,2,1,0:T(8,128)(2,1)S(1)} collective-permute-done((bf16[2,2,128,640]{3,2,1,0:T(8,128)(2,1)S(1)}, bf16[2,2,128,640]{3,2,1,0:T(8,128)(2,1)S(1)}, u32[]{:S(2)}, u32[]{:S(2)}) %collective-permute-start.6) | collective-permute-done | bytes 655392 | tf_op jit(solution)/shard_map/ppermute | solution.py:366
  72.0 1.0 shard_map.79
  73.1 1.9 %collective-permute-start.11 = (bf16[2,128,640]{2,1,0:T(8,128)(2,1)S(1)}, bf16[2,128,640]{2,1,0:T(8,128)(2,1)S(1)}, u32[]{:S(2)}, u32[]{:S(2)}) collective-permute-start(bf16[2,128,640]{2,1,0:T(8,128)(2,1)S(1)} %get-tuple-element.21), channel_id=1, source_target_pairs={{32,96},{33,97},{34,98},{35,99},{36,100},{37,101},{38,102},{39,103... | collective-permute-start | bytes 983048 | tf_op jit(solution)/shard_map/ppermute | solution.py:366
  75.0 5.5 %collective-permute-start.12 = (bf16[2,128,640]{2,1,0:T(8,128)(2,1)S(1)}, bf16[2,128,640]{2,1,0:T(8,128)(2,1)S(1)}, u32[]{:S(2)}, u32[]{:S(2)}) collective-permute-start(bf16[2,128,640]{2,1,0:T(8,128)(2,1)S(1)} %get-tuple-element.22), channel_id=1, source_target_pairs={{0,64},{1,65},{2,66},{3,67},{4,68},{5,69},{6,70},{7,71},{8,72},{9,... | collective-permute-start | bytes 983048 | tf_op jit(solution)/shard_map/ppermute | solution.py:366
  80.5 3.5 %shard_map.81 = bf16[2,128,640]{2,1,0:T(8,128)(2,1)S(1)} custom-call(s32[2]{0:T(128)S(1)} %pad_add_fusion.at_ref, f32[4,2,1152]{2,1,0:T(2,128)S(1)} %reshape.59.bias_ref, bf16[3,128,640]{2,1,0:T(8,128)(2,1)S(1)} %copy-done.2, bf16[3,128,640]{2,1,0:T(8,128)(2,1)S(1)} %collective-permute-done.second.got1, ...), custom_call_target="tpu_custom_call" | custom-call | flops 335544320 | bytes 8000000 | tf_op jit(solution)/shard_map/pallas_call | solution.py:342
  84.0 1.1 collective-permute-done.12.rest_1_
  85.1 3.6 %shard_map.80 = bf16[2,128,640]{2,1,0:T(8,128)(2,1)S(1)} custom-call(s32[2]{0:T(128)S(1)} %pad_add_fusion.at_ref, f32[4,2,1152]{2,1,0:T(2,128)S(1)} %reshape.59.bias_ref, bf16[3,128,640]{2,1,0:T(8,128)(2,1)S(1)} %copy-done.2, bf16[3,128,640]{2,1,0:T(8,128)(2,1)S(1)} %collective-permute-done.second.got1, ...), custom_call_target="tpu_custom_call" | custom-call | flops 335544320 | bytes 8000000 | tf_op jit(solution)/shard_map/pallas_call | solution.py:342
  88.9 17.1 %all_to_all.5.in_ref = bf16[4,128,640]{2,1,0:T(8,128)(2,1)S(1)} all-to-all(bf16[4,128,640]{2,1,0:T(8,128)(2,1)S(1)} %pad_maximum_fusion), channel_id=1, replica_groups={{0,16,32,48},{64,80,96,112},{128,144,160,176},{192,208,224,240},{256,27..., dimensions={0} | all-to-all | bytes 1310720 | tf_op jit(solution)/shard_map/all_to_all | solution.py:437
  105.9 0.9 shard_map.82
  (34 shorter events, 0.8 us)
Async XLA Ops:
  0.0 10.7 %copy-start = (s32[5,32,5]{1,2,0:T(8,128)S(1)}, s32[5,32,5]{1,2,0:T(8,128)}, u32[]{:S(2)}) copy-start(s32[5,32,5]{1,2,0:T(8,128)} %param.10) | copy-start | bytes 9604
  0.0 11.0 %copy-start.5 = (s32[18]{0:T(128)S(1)}, s32[18]{0:T(128)}, u32[]{:S(2)}) copy-start(s32[18]{0:T(128)} %constant.48.clone) | copy-start | bytes 220
  0.0 11.0 %copy-start.4 = (s32[18]{0:T(128)S(1)}, s32[18]{0:T(128)}, u32[]{:S(2)}) copy-start(s32[18]{0:T(128)} %constant.47.clone) | copy-start | bytes 220
  3.1 19.2 %copy-start.3 = (f32[2,18,50]{2,0,1:T(2,128)S(1)}, f32[2,18,50]{2,0,1:T(2,128)}, u32[]{:S(2)}) copy-start(f32[2,18,50]{2,0,1:T(2,128)} %constant.46.clone) | copy-start | bytes 21604
  3.1 8.1 %collective-permute-start = (bf16[3,128,640]{2,1,0:T(8,128)(2,1)}, bf16[3,128,640]{2,1,0:T(8,128)(2,1)S(1)}, u32[]{:S(2)}, u32[]{:S(2)}) collective-permute-start(bf16[3,128,640]{2,1,0:T(8,128)(2,1)} %get-tuple-element.15), channel_id=1, source_target_pairs={{0,16},{1,17},{2,18},{3,19},{4,20},{5,21},{6,22},{7,23},{8,24},{9,... | collective-permute-start | bytes 1474568 | tf_op jit(solution)/shard_map/ppermute | solution.py:366
  5.0 19.3 %collective-permute-start.1 = (bf16[3,128,640]{2,1,0:T(8,128)(2,1)}, bf16[3,128,640]{2,1,0:T(8,128)(2,1)S(1)}, u32[]{:S(2)}, u32[]{:S(2)}) collective-permute-start(bf16[3,128,640]{2,1,0:T(8,128)(2,1)} %get-tuple-element.16), channel_id=1, source_target_pairs={{0,32},{1,33},{2,34},{3,35},{4,36},{5,37},{6,38},{7,39},{8,40},{9,... | collective-permute-start | bytes 1474568 | tf_op jit(solution)/shard_map/ppermute | solution.py:366
  7.6 23.3 %collective-permute-start.2 = (bf16[3,128,640]{2,1,0:T(8,128)(2,1)}, bf16[3,128,640]{2,1,0:T(8,128)(2,1)S(1)}, u32[]{:S(2)}, u32[]{:S(2)}) collective-permute-start(bf16[3,128,640]{2,1,0:T(8,128)(2,1)} %get-tuple-element.17), channel_id=1, source_target_pairs={{0,48},{1,49},{2,50},{3,51},{4,52},{5,53},{6,54},{7,55},{8,56},{9,... | collective-permute-start | bytes 1474568 | tf_op jit(solution)/shard_map/ppermute | solution.py:366
  11.1 1.0 copy-start.1
  13.2 24.2 %collective-permute-start.3 = (bf16[2,2,128,640]{3,2,1,0:T(8,128)(2,1)}, bf16[2,2,128,640]{3,2,1,0:T(8,128)(2,1)S(1)}, u32[]{:S(2)}, u32[]{:S(2)}) collective-permute-start(bf16[2,2,128,640]{3,2,1,0:T(8,128)(2,1)} %shard_map.74.own), channel_id=1, source_target_pairs={{0,1},{1,2},{2,3},{3,0},{4,5},{5,6},{6,7},{7,4},{8,9},{9,10},{10,1... | collective-permute-start | bytes 1966088 | tf_op jit(solution)/shard_map/ppermute | solution.py:366
  16.6 20.9 %collective-permute-start.4 = (bf16[2,2,128,640]{3,2,1,0:T(8,128)(2,1)}, bf16[2,2,128,640]{3,2,1,0:T(8,128)(2,1)S(1)}, u32[]{:S(2)}, u32[]{:S(2)}) collective-permute-start(bf16[2,2,128,640]{3,2,1,0:T(8,128)(2,1)} %shard_map.74.own), channel_id=1, source_target_pairs={{0,3},{1,0},{2,1},{3,2},{4,7},{5,4},{6,5},{7,6},{8,11},{9,8},{10,9... | collective-permute-start | bytes 1966088 | tf_op jit(solution)/shard_map/ppermute | solution.py:366
  20.3 20.3 %collective-permute-start.5 = (bf16[2,2,128,640]{3,2,1,0:T(8,128)(2,1)}, bf16[2,2,128,640]{3,2,1,0:T(8,128)(2,1)S(1)}, u32[]{:S(2)}, u32[]{:S(2)}) collective-permute-start(bf16[2,2,128,640]{3,2,1,0:T(8,128)(2,1)} %shard_map.74.own), channel_id=1, source_target_pairs={{32,96},{33,97},{34,98},{35,99},{36,100},{37,101},{38,102},{39,103... | collective-permute-start | bytes 1966088 | tf_op jit(solution)/shard_map/ppermute | solution.py:366
  31.1 9.5 %copy-start.2 = (bf16[3,128,640]{2,1,0:T(8,128)(2,1)S(1)}, bf16[3,128,640]{2,1,0:T(8,128)(2,1)}, u32[]{:S(2)}) copy-start(bf16[3,128,640]{2,1,0:T(8,128)(2,1)} %get-tuple-element.14.first.got0) | copy-start | bytes 1474564
  31.1 35.1 %collective-permute-start.9 = (bf16[2,2,128,640]{3,2,1,0:T(8,128)(2,1)S(1)}, bf16[2,2,128,640]{3,2,1,0:T(8,128)(2,1)S(1)}, u32[]{:S(2)}, u32[]{:S(2)}) collective-permute-start(bf16[2,2,128,640]{3,2,1,0:T(8,128)(2,1)S(1)} %shard_map.75.after.oth), channel_id=1, source_target_pairs={{3,4},{4,3},{7,8},{8,7},{11,12},{12,11},{19,20},{20,19},{23,24},{2... | collective-permute-start | bytes 1966088 | tf_op jit(solution)/shard_map/ppermute | solution.py:366
  38.3 33.8 %collective-permute-start.6 = (bf16[2,2,128,640]{3,2,1,0:T(8,128)(2,1)S(1)}, bf16[2,2,128,640]{3,2,1,0:T(8,128)(2,1)S(1)}, u32[]{:S(2)}, u32[]{:S(2)}) collective-permute-start(bf16[2,2,128,640]{3,2,1,0:T(8,128)(2,1)S(1)} %shard_map.76.after0), channel_id=1, source_target_pairs={{0,4},{4,8},{7,3},{8,12},{11,7},{15,11},{16,20},{20,24},{23,19},{2... | collective-permute-start | bytes 1966088 | tf_op jit(solution)/shard_map/ppermute | solution.py:366
  44.9 27.1 %collective-permute-start.7 = (bf16[2,2,128,640]{3,2,1,0:T(8,128)(2,1)S(1)}, bf16[2,2,128,640]{3,2,1,0:T(8,128)(2,1)S(1)}, u32[]{:S(2)}, u32[]{:S(2)}) collective-permute-start(bf16[2,2,128,640]{3,2,1,0:T(8,128)(2,1)S(1)} %shard_map.78), channel_id=1, source_target_pairs={{0,1},{1,2},{2,3},{4,5},{5,6},{6,7},{8,9},{9,10},{10,11},{12,13},{... | collective-permute-start | bytes 1966088 | tf_op jit(solution)/shard_map/ppermute | solution.py:366
  47.1 24.9 %collective-permute-start.8 = (bf16[2,2,128,640]{3,2,1,0:T(8,128)(2,1)S(1)}, bf16[2,2,128,640]{3,2,1,0:T(8,128)(2,1)S(1)}, u32[]{:S(2)}, u32[]{:S(2)}) collective-permute-start(bf16[2,2,128,640]{3,2,1,0:T(8,128)(2,1)S(1)} %shard_map.78), channel_id=1, source_target_pairs={{1,0},{2,1},{3,2},{5,4},{6,5},{7,6},{9,8},{10,9},{11,10},{13,12},{... | collective-permute-start | bytes 1966088 | tf_op jit(solution)/shard_map/ppermute | solution.py:366
  48.4 32.1 %collective-permute-start.10 = (bf16[2,2,128,640]{3,2,1,0:T(8,128)(2,1)S(1)}, bf16[2,2,128,640]{3,2,1,0:T(8,128)(2,1)S(1)}, u32[]{:S(2)}, u32[]{:S(2)}) collective-permute-start(bf16[2,2,128,640]{3,2,1,0:T(8,128)(2,1)S(1)} %shard_map.78), channel_id=1, source_target_pairs={{0,64},{1,65},{2,66},{3,67},{4,68},{5,69},{6,70},{7,71},{8,72},{9,... | collective-permute-start | bytes 1966088 | tf_op jit(solution)/shard_map/ppermute | solution.py:366
  73.1 10.9 %collective-permute-start.11 = (bf16[2,128,640]{2,1,0:T(8,128)(2,1)S(1)}, bf16[2,128,640]{2,1,0:T(8,128)(2,1)S(1)}, u32[]{:S(2)}, u32[]{:S(2)}) collective-permute-start(bf16[2,128,640]{2,1,0:T(8,128)(2,1)S(1)} %get-tuple-element.21), channel_id=1, source_target_pairs={{32,96},{33,97},{34,98},{35,99},{36,100},{37,101},{38,102},{39,103... | collective-permute-start | bytes 983048 | tf_op jit(solution)/shard_map/ppermute | solution.py:366
  75.0 10.1 %collective-permute-start.12 = (bf16[2,128,640]{2,1,0:T(8,128)(2,1)S(1)}, bf16[2,128,640]{2,1,0:T(8,128)(2,1)S(1)}, u32[]{:S(2)}, u32[]{:S(2)}) collective-permute-start(bf16[2,128,640]{2,1,0:T(8,128)(2,1)S(1)} %get-tuple-element.22), channel_id=1, source_target_pairs={{0,64},{1,65},{2,66},{3,67},{4,68},{5,69},{6,70},{7,71},{8,72},{9,... | collective-permute-start | bytes 983048 | tf_op jit(solution)/shard_map/ppermute | solution.py:366

commit v5 on v3

--- a/solution.py
+++ b/solution.py
@@ -345,7 +345,7 @@
         out_specs=jax.tree.map(lambda _: VMEM, out_shape),
         out_shape=out_shape,
         scratch_shapes=[pltpu.VMEM(scratch, jnp.bfloat16) for scratch in scratches],
-        compiler_params=pltpu.CompilerParams(vmem_limit_bytes=24 * 2**20),
+        compiler_params=pltpu.CompilerParams(vmem_limit_bytes=18 * 2**20),
         cost_estimate=pl.CostEstimate(
             flops=4 * work * width * length, bytes_accessed=8_000_000,
             transcendentals=work * width * length // HDIM,

time: 107 us -> 107 us (level)
  no operation moved by 1% of the time
where the time goes in v5:
time: 107 us
  starting transfers between devices  38.8 us (36%)
  waiting for transfers between devices  28.7 us (27%)
  Pallas kernels  17.3 us (16%)
  blocking collectives  17.1 us (16%)
  local copies, waits for them, and re-layouts  3.21 us (3%)
  other arithmetic  1.28 us (1%)
    ppermute x13, starting transfers between devices, send(): return lax.ppermute(array, AXES, pairs_of(frame_total, row_total, target))  38.8 us
    ppermute x13, waiting for transfers between devices, send(): return lax.ppermute(array, AXES, pairs_of(frame_total, row_total, target))  28.7 us
    all_to_all x1, blocking collectives, shards(): back = lax.all_to_all(by_frame, 'frame', 0, 0, axis_index_groups=groups)  17.1 us
    pallas_call x3, Pallas kernels, attend(): pl.pallas_call(kernel, in_specs=[SMEM] + [VMEM] * (1 + len(arrays)) + [AN...  11.2 us
    pallas_call x1, Pallas kernels, shards(): pl.pallas_call(pack_kernel, in_specs=[ANY] * 3, out_specs=[VMEM] * GROUP,...  3.02 us
  transfers between devices with their start and end apart: 13, of which 5 were waited for; matrix products, arithmetic and copies ran while one was open for 4% of the time, Pallas kernels for 9%

profile of v5, /device:TPU:240, one launch (start us, length us, event | category | flops | bytes accessed | tf_op | source)
XLA Modules:
  0.0 106.8 jit_solution(3986968332964169098)
XLA Ops:
  0.0 3.0 %shard_map.73 = (bf16[3,128,640]{2,1,0:T(8,128)(2,1)}, bf16[3,128,640]{2,1,0:T(8,128)(2,1)}, bf16[3,128,640]{2,1,0:T(8,128)(2,1)}, bf16[3,128,640]{2,1,0:T(8,128)(2,1)}) custom-call(bf16[128,2560]{1,0:T(8,128)(2,1)} %bitcast.10, bf16[128,2560]{1,0:T(8,128)(2,1)} %bitcast.11, bf16[128,2560]{1,0:T(8,128)(2,1)} %bitcast.12), custom_call_target="tpu_custom_call" | custom-call | tf_op jit(solution)/shard_map/pallas_call | solution.py:368
  3.0 1.9 %collective-permute-start = (bf16[3,128,640]{2,1,0:T(8,128)(2,1)}, bf16[3,128,640]{2,1,0:T(8,128)(2,1)S(1)}, u32[]{:S(2)}, u32[]{:S(2)}) collective-permute-start(bf16[3,128,640]{2,1,0:T(8,128)(2,1)} %get-tuple-element.15), channel_id=1, source_target_pairs={{0,16},{1,17},{2,18},{3,19},{4,20},{5,21},{6,22},{7,23},{8,24},{9,... | collective-permute-start | bytes 1474568 | tf_op jit(solution)/shard_map/ppermute | solution.py:366
  5.0 2.6 %collective-permute-start.1 = (bf16[3,128,640]{2,1,0:T(8,128)(2,1)}, bf16[3,128,640]{2,1,0:T(8,128)(2,1)S(1)}, u32[]{:S(2)}, u32[]{:S(2)}) collective-permute-start(bf16[3,128,640]{2,1,0:T(8,128)(2,1)} %get-tuple-element.16), channel_id=1, source_target_pairs={{0,32},{1,33},{2,34},{3,35},{4,36},{5,37},{6,38},{7,39},{8,40},{9,... | collective-permute-start | bytes 1474568 | tf_op jit(solution)/shard_map/ppermute | solution.py:366
  7.6 3.1 %collective-permute-start.2 = (bf16[3,128,640]{2,1,0:T(8,128)(2,1)}, bf16[3,128,640]{2,1,0:T(8,128)(2,1)S(1)}, u32[]{:S(2)}, u32[]{:S(2)}) collective-permute-start(bf16[3,128,640]{2,1,0:T(8,128)(2,1)} %get-tuple-element.17), channel_id=1, source_target_pairs={{0,48},{1,49},{2,50},{3,51},{4,52},{5,53},{6,54},{7,55},{8,56},{9,... | collective-permute-start | bytes 1474568 | tf_op jit(solution)/shard_map/ppermute | solution.py:366
  11.1 1.0 slice_bitcast_fusion.1
  12.2 0.9 pad_maximum_fusion.own
  13.1 3.4 %collective-permute-start.3 = (bf16[2,2,128,640]{3,2,1,0:T(8,128)(2,1)}, bf16[2,2,128,640]{3,2,1,0:T(8,128)(2,1)S(1)}, u32[]{:S(2)}, u32[]{:S(2)}) collective-permute-start(bf16[2,2,128,640]{3,2,1,0:T(8,128)(2,1)} %pad_maximum_fusion.own), channel_id=1, source_target_pairs={{0,1},{1,2},{2,3},{3,0},{4,5},{5,6},{6,7},{7,4},{8,9},{9,10},{10,1... | collective-permute-start | bytes 1966088 | tf_op jit(solution)/shard_map/ppermute | solution.py:366
  16.5 3.7 %collective-permute-start.4 = (bf16[2,2,128,640]{3,2,1,0:T(8,128)(2,1)}, bf16[2,2,128,640]{3,2,1,0:T(8,128)(2,1)S(1)}, u32[]{:S(2)}, u32[]{:S(2)}) collective-permute-start(bf16[2,2,128,640]{3,2,1,0:T(8,128)(2,1)} %pad_maximum_fusion.own), channel_id=1, source_target_pairs={{0,3},{1,0},{2,1},{3,2},{4,7},{5,4},{6,5},{7,6},{8,11},{9,8},{10,9... | collective-permute-start | bytes 1966088 | tf_op jit(solution)/shard_map/ppermute | solution.py:366
  20.1 1.9 %collective-permute-start.5 = (bf16[2,2,128,640]{3,2,1,0:T(8,128)(2,1)}, bf16[2,2,128,640]{3,2,1,0:T(8,128)(2,1)S(1)}, u32[]{:S(2)}, u32[]{:S(2)}) collective-permute-start(bf16[2,2,128,640]{3,2,1,0:T(8,128)(2,1)} %pad_maximum_fusion.own), channel_id=1, source_target_pairs={{32,96},{33,97},{34,98},{35,99},{36,100},{37,101},{38,102},{39,103... | collective-permute-start | bytes 1966088 | tf_op jit(solution)/shard_map/ppermute | solution.py:366
  22.3 0.7 broadcast_in_dim.21
  23.0 1.0 reshape.59.bias_ref
  24.1 6.7 %collective-permute-done.2.second.got3 = bf16[3,128,640]{2,1,0:T(8,128)(2,1)S(1)} collective-permute-done((bf16[3,128,640]{2,1,0:T(8,128)(2,1)}, bf16[3,128,640]{2,1,0:T(8,128)(2,1)S(1)}, u32[]{:S(2)}, u32[]{:S(2)}) %collective-permute-start.2) | collective-permute-done | bytes 491552 | tf_op jit(solution)/shard_map/ppermute | solution.py:366
  30.8 0.2 shard_map.74.after.oth
  31.1 6.4 %collective-permute-start.9 = (bf16[2,2,128,640]{3,2,1,0:T(8,128)(2,1)S(1)}, bf16[2,2,128,640]{3,2,1,0:T(8,128)(2,1)S(1)}, u32[]{:S(2)}, u32[]{:S(2)}) collective-permute-start(bf16[2,2,128,640]{3,2,1,0:T(8,128)(2,1)S(1)} %shard_map.74.after.oth), channel_id=1, source_target_pairs={{3,4},{4,3},{7,8},{8,7},{11,12},{12,11},{19,20},{20,19},{23,24},{2... | collective-permute-start | bytes 1966088 | tf_op jit(solution)/shard_map/ppermute | solution.py:366
  37.5 0.8 shard_map.75.after0
  38.2 1.3 %collective-permute-start.6 = (bf16[2,2,128,640]{3,2,1,0:T(8,128)(2,1)S(1)}, bf16[2,2,128,640]{3,2,1,0:T(8,128)(2,1)S(1)}, u32[]{:S(2)}, u32[]{:S(2)}) collective-permute-start(bf16[2,2,128,640]{3,2,1,0:T(8,128)(2,1)S(1)} %shard_map.75.after0), channel_id=1, source_target_pairs={{0,4},{4,8},{7,3},{8,12},{11,7},{15,11},{16,20},{20,24},{23,19},{2... | collective-permute-start | bytes 1966088 | tf_op jit(solution)/shard_map/ppermute | solution.py:366
  39.5 0.9 collective-permute-done.5.after1.z_own
  40.5 4.0 %shard_map.76 = (f32[4,128,640]{2,1,0:T(8,128)S(1)}, f32[4,128,640]{2,1,0:T(8,128)S(1)}, f32[4,128,640]{2,1,0:T(8,128)S(1)}) custom-call(s32[2]{0:T(128)S(1)} %pad_add_fusion.at_ref, f32[4,2,1152]{2,1,0:T(2,128)S(1)} %reshape.59.bias_ref, bf16[3,128,640]{2,1,0:T(8,128)(2,1)S(1)} %copy-done.1, bf16[3,128,640]{2,1,0:T(8,128)(2,1)S(1)} %collective-permute-done.got1, ...), custom_call_target="tpu_custom_call" | custom-call | flops 587202560 | bytes 8000000 | tf_op jit(solution)/shard_map/pallas_call | solution.py:342
  44.5 0.2 shard_map.77
  44.7 2.2 %collective-permute-start.7 = (bf16[2,2,128,640]{3,2,1,0:T(8,128)(2,1)S(1)}, bf16[2,2,128,640]{3,2,1,0:T(8,128)(2,1)S(1)}, u32[]{:S(2)}, u32[]{:S(2)}) collective-permute-start(bf16[2,2,128,640]{3,2,1,0:T(8,128)(2,1)S(1)} %shard_map.77), channel_id=1, source_target_pairs={{0,1},{1,2},{2,3},{4,5},{5,6},{6,7},{8,9},{9,10},{10,11},{12,13},{... | collective-permute-start | bytes 1966088 | tf_op jit(solution)/shard_map/ppermute | solution.py:366
  47.0 1.3 %collective-permute-start.8 = (bf16[2,2,128,640]{3,2,1,0:T(8,128)(2,1)S(1)}, bf16[2,2,128,640]{3,2,1,0:T(8,128)(2,1)S(1)}, u32[]{:S(2)}, u32[]{:S(2)}) collective-permute-start(bf16[2,2,128,640]{3,2,1,0:T(8,128)(2,1)S(1)} %shard_map.77), channel_id=1, source_target_pairs={{1,0},{2,1},{3,2},{5,4},{6,5},{7,6},{9,8},{10,9},{11,10},{13,12},{... | collective-permute-start | bytes 1966088 | tf_op jit(solution)/shard_map/ppermute | solution.py:366
  48.3 3.7 %collective-permute-start.10 = (bf16[2,2,128,640]{3,2,1,0:T(8,128)(2,1)S(1)}, bf16[2,2,128,640]{3,2,1,0:T(8,128)(2,1)S(1)}, u32[]{:S(2)}, u32[]{:S(2)}) collective-permute-start(bf16[2,2,128,640]{3,2,1,0:T(8,128)(2,1)S(1)} %shard_map.77), channel_id=1, source_target_pairs={{0,64},{1,65},{2,66},{3,67},{4,68},{5,69},{6,70},{7,71},{8,72},{9,... | collective-permute-start | bytes 1966088 | tf_op jit(solution)/shard_map/ppermute | solution.py:366
  52.0 14.2 %collective-permute-done.9.direct = bf16[2,2,128,640]{3,2,1,0:T(8,128)(2,1)S(1)} collective-permute-done((bf16[2,2,128,640]{3,2,1,0:T(8,128)(2,1)S(1)}, bf16[2,2,128,640]{3,2,1,0:T(8,128)(2,1)S(1)}, u32[]{:S(2)}, u32[]{:S(2)}) %collective-permute-start.9) | collective-permute-done | bytes 655392 | tf_op jit(solution)/shard_map/ppermute | solution.py:366
  66.1 5.9 %collective-permute-done.6.second = bf16[2,2,128,640]{3,2,1,0:T(8,128)(2,1)S(1)} collective-permute-done((bf16[2,2,128,640]{3,2,1,0:T(8,128)(2,1)S(1)}, bf16[2,2,128,640]{3,2,1,0:T(8,128)(2,1)S(1)}, u32[]{:S(2)}, u32[]{:S(2)}) %collective-permute-start.6) | collective-permute-done | bytes 655392 | tf_op jit(solution)/shard_map/ppermute | solution.py:366
  72.0 1.0 shard_map.78
  73.0 1.9 %collective-permute-start.11 = (bf16[2,128,640]{2,1,0:T(8,128)(2,1)S(1)}, bf16[2,128,640]{2,1,0:T(8,128)(2,1)S(1)}, u32[]{:S(2)}, u32[]{:S(2)}) collective-permute-start(bf16[2,128,640]{2,1,0:T(8,128)(2,1)S(1)} %get-tuple-element.21), channel_id=1, source_target_pairs={{32,96},{33,97},{34,98},{35,99},{36,100},{37,101},{38,102},{39,103... | collective-permute-start | bytes 983048 | tf_op jit(solution)/shard_map/ppermute | solution.py:366
  75.0 5.5 %collective-permute-start.12 = (bf16[2,128,640]{2,1,0:T(8,128)(2,1)S(1)}, bf16[2,128,640]{2,1,0:T(8,128)(2,1)S(1)}, u32[]{:S(2)}, u32[]{:S(2)}) collective-permute-start(bf16[2,128,640]{2,1,0:T(8,128)(2,1)S(1)} %get-tuple-element.22), channel_id=1, source_target_pairs={{0,64},{1,65},{2,66},{3,67},{4,68},{5,69},{6,70},{7,71},{8,72},{9,... | collective-permute-start | bytes 983048 | tf_op jit(solution)/shard_map/ppermute | solution.py:366
  80.5 3.5 %shard_map.80 = bf16[2,128,640]{2,1,0:T(8,128)(2,1)S(1)} custom-call(s32[2]{0:T(128)S(1)} %pad_add_fusion.at_ref, f32[4,2,1152]{2,1,0:T(2,128)S(1)} %reshape.59.bias_ref, bf16[3,128,640]{2,1,0:T(8,128)(2,1)S(1)} %copy-done.1, bf16[3,128,640]{2,1,0:T(8,128)(2,1)S(1)} %collective-permute-done.got1, bf16[3,128,640]{2,1,0:T(8,128)(2,1)S(1)} %collective-permute-done.1.first.got2, ...), custom_call_target="tpu_custom_call" | custom-call | flops 335544320 | bytes 8000000 | tf_op jit(solution)/shard_map/pallas_call | solution.py:342
  84.0 1.1 collective-permute-done.12.rest_1_
  85.0 3.7 %shard_map.79 = bf16[2,128,640]{2,1,0:T(8,128)(2,1)S(1)} custom-call(s32[2]{0:T(128)S(1)} %pad_add_fusion.at_ref, f32[4,2,1152]{2,1,0:T(2,128)S(1)} %reshape.59.bias_ref, bf16[3,128,640]{2,1,0:T(8,128)(2,1)S(1)} %copy-done.1, bf16[3,128,640]{2,1,0:T(8,128)(2,1)S(1)} %collective-permute-done.got1, bf16[3,128,640]{2,1,0:T(8,128)(2,1)S(1)} %collective-permute-done.1.first.got2, ...), custom_call_target="tpu_custom_call" | custom-call | flops 335544320 | bytes 8000000 | tf_op jit(solution)/shard_map/pallas_call | solution.py:342
  88.8 17.1 %all_to_all.5.in_ref = bf16[4,128,640]{2,1,0:T(8,128)(2,1)S(1)} all-to-all(bf16[4,128,640]{2,1,0:T(8,128)(2,1)S(1)} %pad_maximum_fusion.1), channel_id=1, replica_groups={{0,16,32,48},{64,80,96,112},{128,144,160,176},{192,208,224,240},{256,27..., dimensions={0} | all-to-all | bytes 1310720 | tf_op jit(solution)/shard_map/all_to_all | solution.py:437
  105.9 0.9 shard_map.81
  (34 shorter events, 0.9 us)
Async XLA Ops:
  0.0 10.7 %copy-start = (s32[5,32,5]{1,2,0:T(8,128)S(1)}, s32[5,32,5]{1,2,0:T(8,128)}, u32[]{:S(2)}) copy-start(s32[5,32,5]{1,2,0:T(8,128)} %param.10) | copy-start | bytes 9604
  0.0 10.7 %copy-start.4 = (s32[18]{0:T(128)S(1)}, s32[18]{0:T(128)}, u32[]{:S(2)}) copy-start(s32[18]{0:T(128)} %constant.48.clone) | copy-start | bytes 220
  0.0 11.0 %copy-start.3 = (s32[18]{0:T(128)S(1)}, s32[18]{0:T(128)}, u32[]{:S(2)}) copy-start(s32[18]{0:T(128)} %constant.47.clone) | copy-start | bytes 220
  3.0 9.1 %collective-permute-start = (bf16[3,128,640]{2,1,0:T(8,128)(2,1)}, bf16[3,128,640]{2,1,0:T(8,128)(2,1)S(1)}, u32[]{:S(2)}, u32[]{:S(2)}) collective-permute-start(bf16[3,128,640]{2,1,0:T(8,128)(2,1)} %get-tuple-element.15), channel_id=1, source_target_pairs={{0,16},{1,17},{2,18},{3,19},{4,20},{5,21},{6,22},{7,23},{8,24},{9,... | collective-permute-start | bytes 1474568 | tf_op jit(solution)/shard_map/ppermute | solution.py:366
  5.0 19.1 %collective-permute-start.1 = (bf16[3,128,640]{2,1,0:T(8,128)(2,1)}, bf16[3,128,640]{2,1,0:T(8,128)(2,1)S(1)}, u32[]{:S(2)}, u32[]{:S(2)}) collective-permute-start(bf16[3,128,640]{2,1,0:T(8,128)(2,1)} %get-tuple-element.16), channel_id=1, source_target_pairs={{0,32},{1,33},{2,34},{3,35},{4,36},{5,37},{6,38},{7,39},{8,40},{9,... | collective-permute-start | bytes 1474568 | tf_op jit(solution)/shard_map/ppermute | solution.py:366
  7.6 23.3 %collective-permute-start.2 = (bf16[3,128,640]{2,1,0:T(8,128)(2,1)}, bf16[3,128,640]{2,1,0:T(8,128)(2,1)S(1)}, u32[]{:S(2)}, u32[]{:S(2)}) collective-permute-start(bf16[3,128,640]{2,1,0:T(8,128)(2,1)} %get-tuple-element.17), channel_id=1, source_target_pairs={{0,48},{1,49},{2,50},{3,51},{4,52},{5,53},{6,54},{7,55},{8,56},{9,... | collective-permute-start | bytes 1474568 | tf_op jit(solution)/shard_map/ppermute | solution.py:366
  11.1 11.0 %copy-start.2 = (f32[2,18,50]{2,0,1:T(2,128)S(1)}, f32[2,18,50]{2,0,1:T(2,128)}, u32[]{:S(2)}) copy-start(f32[2,18,50]{2,0,1:T(2,128)} %constant.46.clone) | copy-start | bytes 21604
  13.1 24.4 %collective-permute-start.3 = (bf16[2,2,128,640]{3,2,1,0:T(8,128)(2,1)}, bf16[2,2,128,640]{3,2,1,0:T(8,128)(2,1)S(1)}, u32[]{:S(2)}, u32[]{:S(2)}) collective-permute-start(bf16[2,2,128,640]{3,2,1,0:T(8,128)(2,1)} %pad_maximum_fusion.own), channel_id=1, source_target_pairs={{0,1},{1,2},{2,3},{3,0},{4,5},{5,6},{6,7},{7,4},{8,9},{9,10},{10,1... | collective-permute-start | bytes 1966088 | tf_op jit(solution)/shard_map/ppermute | solution.py:366
  16.5 21.0 %collective-permute-start.4 = (bf16[2,2,128,640]{3,2,1,0:T(8,128)(2,1)}, bf16[2,2,128,640]{3,2,1,0:T(8,128)(2,1)S(1)}, u32[]{:S(2)}, u32[]{:S(2)}) collective-permute-start(bf16[2,2,128,640]{3,2,1,0:T(8,128)(2,1)} %pad_maximum_fusion.own), channel_id=1, source_target_pairs={{0,3},{1,0},{2,1},{3,2},{4,7},{5,4},{6,5},{7,6},{8,11},{9,8},{10,9... | collective-permute-start | bytes 1966088 | tf_op jit(solution)/shard_map/ppermute | solution.py:366
  20.1 20.3 %collective-permute-start.5 = (bf16[2,2,128,640]{3,2,1,0:T(8,128)(2,1)}, bf16[2,2,128,640]{3,2,1,0:T(8,128)(2,1)S(1)}, u32[]{:S(2)}, u32[]{:S(2)}) collective-permute-start(bf16[2,2,128,640]{3,2,1,0:T(8,128)(2,1)} %pad_maximum_fusion.own), channel_id=1, source_target_pairs={{32,96},{33,97},{34,98},{35,99},{36,100},{37,101},{38,102},{39,103... | collective-permute-start | bytes 1966088 | tf_op jit(solution)/shard_map/ppermute | solution.py:366
  31.1 9.4 %copy-start.1 = (bf16[3,128,640]{2,1,0:T(8,128)(2,1)S(1)}, bf16[3,128,640]{2,1,0:T(8,128)(2,1)}, u32[]{:S(2)}) copy-start(bf16[3,128,640]{2,1,0:T(8,128)(2,1)} %get-tuple-element.14.got0) | copy-start | bytes 1474564
  31.1 35.1 %collective-permute-start.9 = (bf16[2,2,128,640]{3,2,1,0:T(8,128)(2,1)S(1)}, bf16[2,2,128,640]{3,2,1,0:T(8,128)(2,1)S(1)}, u32[]{:S(2)}, u32[]{:S(2)}) collective-permute-start(bf16[2,2,128,640]{3,2,1,0:T(8,128)(2,1)S(1)} %shard_map.74.after.oth), channel_id=1, source_target_pairs={{3,4},{4,3},{7,8},{8,7},{11,12},{12,11},{19,20},{20,19},{23,24},{2... | collective-permute-start | bytes 1966088 | tf_op jit(solution)/shard_map/ppermute | solution.py:366
  38.2 33.8 %collective-permute-start.6 = (bf16[2,2,128,640]{3,2,1,0:T(8,128)(2,1)S(1)}, bf16[2,2,128,640]{3,2,1,0:T(8,128)(2,1)S(1)}, u32[]{:S(2)}, u32[]{:S(2)}) collective-permute-start(bf16[2,2,128,640]{3,2,1,0:T(8,128)(2,1)S(1)} %shard_map.75.after0), channel_id=1, source_target_pairs={{0,4},{4,8},{7,3},{8,12},{11,7},{15,11},{16,20},{20,24},{23,19},{2... | collective-permute-start | bytes 1966088 | tf_op jit(solution)/shard_map/ppermute | solution.py:366
  44.7 27.3 %collective-permute-start.7 = (bf16[2,2,128,640]{3,2,1,0:T(8,128)(2,1)S(1)}, bf16[2,2,128,640]{3,2,1,0:T(8,128)(2,1)S(1)}, u32[]{:S(2)}, u32[]{:S(2)}) collective-permute-start(bf16[2,2,128,640]{3,2,1,0:T(8,128)(2,1)S(1)} %shard_map.77), channel_id=1, source_target_pairs={{0,1},{1,2},{2,3},{4,5},{5,6},{6,7},{8,9},{9,10},{10,11},{12,13},{... | collective-permute-start | bytes 1966088 | tf_op jit(solution)/shard_map/ppermute | solution.py:366
  47.0 25.0 %collective-permute-start.8 = (bf16[2,2,128,640]{3,2,1,0:T(8,128)(2,1)S(1)}, bf16[2,2,128,640]{3,2,1,0:T(8,128)(2,1)S(1)}, u32[]{:S(2)}, u32[]{:S(2)}) collective-permute-start(bf16[2,2,128,640]{3,2,1,0:T(8,128)(2,1)S(1)} %shard_map.77), channel_id=1, source_target_pairs={{1,0},{2,1},{3,2},{5,4},{6,5},{7,6},{9,8},{10,9},{11,10},{13,12},{... | collective-permute-start | bytes 1966088 | tf_op jit(solution)/shard_map/ppermute | solution.py:366
  48.3 32.2 %collective-permute-start.10 = (bf16[2,2,128,640]{3,2,1,0:T(8,128)(2,1)S(1)}, bf16[2,2,128,640]{3,2,1,0:T(8,128)(2,1)S(1)}, u32[]{:S(2)}, u32[]{:S(2)}) collective-permute-start(bf16[2,2,128,640]{3,2,1,0:T(8,128)(2,1)S(1)} %shard_map.77), channel_id=1, source_target_pairs={{0,64},{1,65},{2,66},{3,67},{4,68},{5,69},{6,70},{7,71},{8,72},{9,... | collective-permute-start | bytes 1966088 | tf_op jit(solution)/shard_map/ppermute | solution.py:366
  73.0 10.9 %collective-permute-start.11 = (bf16[2,128,640]{2,1,0:T(8,128)(2,1)S(1)}, bf16[2,128,640]{2,1,0:T(8,128)(2,1)S(1)}, u32[]{:S(2)}, u32[]{:S(2)}) collective-permute-start(bf16[2,128,640]{2,1,0:T(8,128)(2,1)S(1)} %get-tuple-element.21), channel_id=1, source_target_pairs={{32,96},{33,97},{34,98},{35,99},{36,100},{37,101},{38,102},{39,103... | collective-permute-start | bytes 983048 | tf_op jit(solution)/shard_map/ppermute | solution.py:366
  75.0 10.1 %collective-permute-start.12 = (bf16[2,128,640]{2,1,0:T(8,128)(2,1)S(1)}, bf16[2,128,640]{2,1,0:T(8,128)(2,1)S(1)}, u32[]{:S(2)}, u32[]{:S(2)}) collective-permute-start(bf16[2,128,640]{2,1,0:T(8,128)(2,1)S(1)} %get-tuple-element.22), channel_id=1, source_target_pairs={{0,64},{1,65},{2,66},{3,67},{4,68},{5,69},{6,70},{7,71},{8,72},{9,... | collective-permute-start | bytes 983048 | tf_op jit(solution)/shard_map/ppermute | solution.py:366
